TPU v7x, 32 devices: a whole 2x2x4 slice. The times are simulated.
32 devices in a mesh: row: 8 (over z, x), col: 4 (over y, core).
Axes of the slice: x: 2, y: 2, z: 4, core: 2. Of those that a mesh axis runs over, the one named last changes fastest.
Arguments:
- strips: bfloat16 [160, 8, 4, 64, 512], P('col', 'row'), may hold values from -6 to 6
- pair_counts: int32 [160, 8, 2], P('col', 'row'), may hold values from 0 to 5, as said below
- pair_offsets: int32 [160, 8, 2], P('col', 'row'), may hold values from 0 to 63
- tile_stiffness: float32 [160, 8], P('col', 'row'), may hold values from 0.1 to 1
- anchor: float32 [160, 8, 896], P('col', 'row'), may hold values from 0.02 to 0.2
Outputs:
- match_terms: float32 [160, 8, 2, 3, 8], P('col', 'row')
- positions: float32 [160, 8, 2, 896], P('col', 'row')
- residual: float32 [160, 8, 2, 896], P('col', 'row')
Inputs may be any that keep to these rules, and one draw needn't show every extreme that they name: `pair_counts`: entry [r, c, 0] belongs to the pair of tiles (r, c) and (r, c + 1), entry [r, c, 1] to tiles (r, c) and (r + 1, c); it is 0 where the second tile does not exist. The 40 tiles of one device (40 consecutive tile rows of one tile column) hold at most 400 valid blocks in all, and some device holds exactly 400.
All inputs are finite; a program needn't handle non-finite values.
Results may differ from a plain program's by a relative error of at most 0.0082.
Values may be sent and summed in bfloat16 or wider, within the bound.
A program may use at most 128 MiB of HBM per device.

v0:
```python
import math

import jax
import jax.numpy as jnp
import numpy as np
from jax import lax
from jax.experimental import pallas as pl
from jax.experimental.pallas import tpu as pltpu
from jax.sharding import PartitionSpec as P

MESH_Y = 28
MESH_X = 32
PATCH = 64
MOST = 5
GROUP = 4
WIDE = 384
PACKED = 2 * MOST * PATCH
SMALL_WEIGHT = 1e-06
NODE_GAP = 16.0
HIGHEST_PREC = lax.Precision.HIGHEST


def tables():
    line = np.arange(PATCH)
    angles = (line[:, None] * line[None, :] % PATCH) * (2.0 * math.pi / PATCH)
    cosine, sine = np.cos(angles), np.sin(angles)
    two = np.eye(2)
    cos2, sin2 = np.kron(two, cosine), np.kron(two, sine)
    depth = np.concatenate([cosine, -sine], axis=0)
    length = np.block([[cos2, -sin2], [sin2, cos2]])
    back_length = np.block([[cos2, sin2], [-sin2, cos2]])
    back_depth = np.concatenate([cosine, -sine], axis=1)
    return [jnp.asarray(t, jnp.bfloat16) for t in (depth, length, back_length, back_depth)]


def pack_two(a, b):
    tail = jnp.concatenate([a[:, 256:320], b[:, 256:320]], axis=1)
    return jnp.concatenate([a[:, :256], b[:, :256], tail], axis=1)


def block_sums(first, second, depth_ref, length_ref, back_length_ref, back_depth_ref):
    count = first.shape[1] // 128
    depth_table = depth_ref[...]

    def by_rows(strip):
        half = jnp.dot(depth_table, strip, preferred_element_type=jnp.float32).astype(jnp.bfloat16)
        return [
            jnp.concatenate([half[:64, 128 * j : 128 * j + 128], half[64:, 128 * j : 128 * j + 128]], axis=1)
            for j in range(count)
        ]

    rows = jnp.concatenate(by_rows(first) + by_rows(second), axis=0)
    spec = jnp.dot(rows, length_ref[...], preferred_element_type=jnp.float32)
    half_rows = 64 * count
    ar, ai = spec[:half_rows, :128], spec[:half_rows, 128:]
    br, bi = spec[half_rows:, :128], spec[half_rows:, 128:]
    inverse = 1.0 / (0.5 * (ar * ar + ai * ai + br * br + bi * bi) + 1.0)
    cross_real = ((ar * br + ai * bi) * inverse).astype(jnp.bfloat16)
    cross_imag = ((ai * br - ar * bi) * inverse).astype(jnp.bfloat16)
    cross = jnp.concatenate([cross_real, cross_imag], axis=1)
    back = jnp.dot(cross, back_length_ref[...], preferred_element_type=jnp.float32).astype(jnp.bfloat16)
    columns = jnp.concatenate(
        [
            jnp.concatenate([back[64 * j : 64 * j + 64, :128], back[64 * j : 64 * j + 64, 128:]], axis=0)
            for j in range(count)
        ],
        axis=1,
    )
    surface = jnp.dot(back_depth_ref[...], columns, preferred_element_type=jnp.float32)
    power = surface * surface
    row_id = lax.broadcasted_iota(jnp.int32, (64, 1), 0)
    depth_offset = ((row_id + 32) % 64 - 32).astype(jnp.float32)
    plain = jnp.sum(power, axis=0, keepdims=True)
    deep = jnp.sum(power * depth_offset, axis=0, keepdims=True)
    plain = jnp.concatenate([plain[:, 128 * j : 128 * j + 128] for j in range(count)], axis=0)
    deep = jnp.concatenate([deep[:, 128 * j : 128 * j + 128] for j in range(count)], axis=0)
    lane = lax.broadcasted_iota(jnp.int32, (count, 128), 1)
    along = plain * ((lane % 64 + 32) % 64 - 32).astype(jnp.float32)
    low = lane < 64
    out = jnp.zeros((count, 128), jnp.float32)
    scale = 1.0 / float(PATCH**4)
    for k, value in enumerate((plain, deep, along)):
        even = jnp.sum(jnp.where(low, value, 0.0), axis=1, keepdims=True) * scale
        odd = jnp.sum(jnp.where(low, 0.0, value), axis=1, keepdims=True) * scale
        out = jnp.where(lane == 2 * k, even, out)
        out = jnp.where(lane == 2 * k + 1, odd, out)
    return out


def south_kernel(first_ref, top_ref, below_ref, next_ref, d_ref, l_ref, bl_ref, bd_ref, out_ref):
    last = pl.program_id(0) == pl.num_programs(0) - 1
    lower = jnp.where(last, next_ref[0], below_ref[0])
    first = jnp.concatenate([pack_two(first_ref[0], first_ref[1]), pack_two(first_ref[2], first_ref[3])], axis=1)
    second = jnp.concatenate([pack_two(top_ref[1], top_ref[2]), pack_two(top_ref[3], lower)], axis=1)
    out_ref[0] = block_sums(first, second, d_ref, l_ref, bl_ref, bd_ref)


def east_kernel(first_ref, second_ref, d_ref, l_ref, bl_ref, bd_ref, out_ref):
    first = jnp.concatenate([pack_two(first_ref[0], first_ref[1]), pack_two(first_ref[2], first_ref[3])], axis=1)
    second = jnp.concatenate([second_ref[0], second_ref[1]], axis=1)
    out_ref[0] = block_sums(first, second, d_ref, l_ref, bl_ref, bd_ref)


def pack_kernel(left_ref, out_ref):
    out_ref[0] = pack_two(left_ref[0], left_ref[1])
    out_ref[1] = pack_two(left_ref[2], left_ref[3])


def strip_spec(side, start=0):
    return pl.BlockSpec((GROUP, None, None, PATCH, WIDE), lambda i: (i + start, 0, side, 0, 0))


def table_specs():
    return [
        pl.BlockSpec((128, 64), lambda i: (0, 0)),
        pl.BlockSpec((256, 256), lambda i: (0, 0)),
        pl.BlockSpec((256, 256), lambda i: (0, 0)),
        pl.BlockSpec((64, 128), lambda i: (0, 0)),
    ]


PARAMS = pltpu.CompilerParams(vmem_limit_bytes=32 * 1024 * 1024)


def sums_shape(groups):
    return jax.ShapeDtypeStruct((groups, 2 * MOST, 128), jnp.float32)


SUMS_SPEC = pl.BlockSpec((1, 2 * MOST, 128), lambda i: (i, 0, 0))


def cost(groups):
    return pl.CostEstimate(flops=groups * 300_000_000, bytes_accessed=groups * 400_000, transcendentals=groups * 81920)


def pack_left(strips, start, groups):
    return pl.pallas_call(
        pack_kernel,
        grid=(groups,),
        in_specs=[strip_spec(0, start)],
        out_specs=pl.BlockSpec((2, PATCH, PACKED), lambda i: (i, 0, 0)),
        out_shape=jax.ShapeDtypeStruct((2 * groups, PATCH, PACKED), jnp.bfloat16),
        compiler_params=PARAMS,
    )(strips)


def south_sums(strips, next_top, table_list):
    tiles = strips.shape[0]
    groups = tiles // GROUP
    below = pl.BlockSpec(
        (1, None, None, PATCH, WIDE),
        lambda i: (jnp.minimum(GROUP * i + GROUP, tiles - 1), 0, 1, 0, 0),
    )
    return pl.pallas_call(
        south_kernel,
        grid=(groups,),
        in_specs=[strip_spec(2), strip_spec(1), below, pl.BlockSpec((1, PATCH, WIDE), lambda i: (0, 0, 0))]
        + table_specs(),
        out_specs=SUMS_SPEC,
        out_shape=sums_shape(groups),
        compiler_params=PARAMS,
        cost_estimate=cost(groups),
    )(strips, strips, strips, next_top, *table_list)


def east_sums(strips, packed, start, table_list):
    groups = packed.shape[0] // 2
    return pl.pallas_call(
        east_kernel,
        grid=(groups,),
        in_specs=[strip_spec(3, start), pl.BlockSpec((2, PATCH, PACKED), lambda i: (i, 0, 0))] + table_specs(),
        out_specs=SUMS_SPEC,
        out_shape=sums_shape(groups),
        compiler_params=PARAMS,
        cost_estimate=cost(groups),
    )(strips, packed, *table_list)


def unpack_sums(sums):
    groups = sums.shape[0]
    sums = sums[:, :, :6].reshape(groups, 2, MOST, 3, 2)
    main = sums[:, :, :4].reshape(groups, 2, 2, 2, 3, 2).transpose(0, 1, 2, 4, 3, 5).reshape(groups * 4, 3, 4)
    tail = sums[:, :, 4].transpose(0, 1, 3, 2).reshape(groups * 4, 3, 1)
    return jnp.concatenate([main, tail, jnp.zeros((groups * 4, 3, 3), jnp.float32)], axis=2)


def passed_along(x, axis, by):
    peers = lax.axis_size(axis)
    pairs = [(i, i + by) for i in range(peers) if 0 <= i + by < peers]
    return lax.ppermute(x, axis, pairs)


def edge_selection():
    chosen = np.zeros((MESH_Y * MESH_X, 128), np.float32)
    for i in range(MESH_Y):
        chosen[MESH_X * i, i] = 1.0
        chosen[MESH_X * i + MESH_X - 1, 32 + i] = 1.0
    for j in range(MESH_X):
        chosen[j, 64 + j] = 1.0
        chosen[MESH_X * (MESH_Y - 1) + j, 96 + j] = 1.0
    return chosen


def cg_weights(moments):
    def dot(p, q):
        return sum(
            a * b * moments[i + j]
            for i, a in enumerate(p)
            for j, b in enumerate(q)
            if a is not None and b is not None
        )

    def add(p, scale, q):
        size = max(len(p), len(q))
        p, q = list(p) + [None] * (size - len(p)), list(q) + [None] * (size - len(q))
        return [a if b is None else scale * b if a is None else a + scale * b for a, b in zip(p, q)]

    one = jnp.ones_like(moments[0])
    residual, direction, positions = [one], [one], [None]
    norm = moments[0]
    for iteration in range(3):
        image = [None] + direction
        alpha = norm / dot(direction, image)
        positions = add(positions, alpha, direction)
        residual = add(residual, -alpha, image)
        if iteration < 2:
            norm_next = dot(residual, residual)
            direction = add(residual, norm_next / norm, direction)
            norm = norm_next
    return positions, residual


def cg_kernel(
    rows, cols, terms_ref, stiff_ref, anchor_ref, pick_ref, place_ref, positions_ref, residual_ref,
    pair_send, pair_recv, edge_send, edge_recv, basis, part, part_row, part_col,
    pair_ssem, pair_rsem, edge_ssem, edge_rsem, row_ssem, row_rsem, col_ssem, col_rsem,
):
    my_row, my_col = lax.axis_index("row"), lax.axis_index("col")
    tiles = terms_ref.shape[0]

    def on_row(by):
        return (lax.rem(my_row + by + rows, rows), my_col)

    def on_col(by):
        return (my_row, lax.rem(my_col + by + cols, cols))

    barrier = pltpu.get_barrier_semaphore()
    for by in range(1, rows):
        pl.semaphore_signal(barrier, inc=1, device_id=on_row(by), device_id_type=pl.DeviceIdType.MESH)
    for by in range(1, cols):
        pl.semaphore_signal(barrier, inc=1, device_id=on_col(by), device_id_type=pl.DeviceIdType.MESH)

    def send(source, target, ssem, rsem, device):
        copy = pltpu.make_async_remote_copy(
            src_ref=source, dst_ref=target, send_sem=ssem, recv_sem=rsem,
            device_id=device, device_id_type=pl.DeviceIdType.MESH,
        )
        copy.start()
        return copy

    lane = lax.broadcasted_iota(jnp.int32, (tiles, 128), 1)
    tile_id = lax.broadcasted_iota(jnp.int32, (tiles, 128), 0)
    node = lane % 32
    group = lane // 32
    own = (group % 2) == 1
    node_count = jnp.where(group < 2, MESH_Y, MESH_X)
    inside = own & (node < node_count)
    linked = own & (node < node_count - 1)

    def term(k):
        return jnp.where(group < 2, terms_ref[:, k : k + 1], terms_ref[:, 24 + k : 25 + k])

    offset = jnp.where(group < 2, terms_ref[:, 48:49], terms_ref[:, 49:50])
    node_pos = NODE_GAP * node.astype(jnp.float32) + NODE_GAP / 2
    zero = jnp.zeros((tiles, 128), jnp.float32)
    self_term, link_term, force_x, force_y = zero, zero, zero, zero
    for k in range(MOST):
        centre = offset + float(PATCH * k + PATCH // 2)
        tent = jnp.maximum(0.0, 1.0 - jnp.abs(centre - node_pos) / NODE_GAP)
        after = jnp.maximum(0.0, 1.0 - jnp.abs(centre - node_pos - NODE_GAP) / NODE_GAP)
        weighted = term(k) * tent
        self_term += weighted * tent
        link_term += weighted * after
        force_x += weighted * term(8 + k)
        force_y += weighted * term(16 + k)
    pair_send[0] = jnp.where(inside, self_term, 0.0)
    pair_send[1] = jnp.where(linked, link_term, 0.0)
    pair_send[2] = jnp.where(inside, force_x, 0.0)
    pair_send[3] = jnp.where(inside, force_y, 0.0)
    pl.semaphore_wait(barrier, rows + cols - 2)
    copies = [
        send(pair_send, pair_recv.at[0], pair_ssem.at[0], pair_rsem.at[0], on_row(1)),
        send(pair_send, pair_recv.at[1], pair_ssem.at[1], pair_rsem.at[1], on_col(1)),
    ]
    for copy in copies:
        copy.wait()

    def partners(west, east, own_part, north, south):
        above = jnp.where(tile_id == 0, north[tiles - 1 : tiles], pltpu.roll(own_part, 1, 0))
        low = pltpu.roll(jnp.where(group == 1, west, above), 96, 1)
        if east is None:
            return jnp.where(own, 0.0, low)
        below = jnp.where(tile_id == tiles - 1, south[0:1], pltpu.roll(own_part, tiles - 1, 0))
        high = pltpu.roll(jnp.where(group == 0, east, below), 32, 1)
        return jnp.where(own, high, low)

    others = [partners(pair_recv[0, c], None, pair_send[c], pair_recv[1, c], None) for c in range(4)]
    self_term = pair_send[0] + others[0]
    link_term = pair_send[1] + others[1]
    self_both = jnp.concatenate([self_term, self_term], axis=0)
    link_both = jnp.concatenate([link_term, link_term], axis=0)
    force = jnp.concatenate([pair_send[2] - others[2], pair_send[3] - others[3]], axis=0)

    def expand(values):
        return jnp.dot(values, place_ref[...], preferred_element_type=jnp.float32, precision=HIGHEST_PREC)

    nodes = MESH_Y * MESH_X
    spot = lax.broadcasted_iota(jnp.int32, (1, nodes), 1)
    column = spot % MESH_X
    keep_left = (column > 0).astype(jnp.float32)
    keep_right = (column < MESH_X - 1).astype(jnp.float32)
    keep_up = (spot >= MESH_X).astype(jnp.float32)
    keep_down = (spot < nodes - MESH_X).astype(jnp.float32)
    degree = keep_left + keep_right + keep_up + keep_down
    stiff = jnp.concatenate([stiff_ref[...], stiff_ref[...]], axis=0)
    anchor = jnp.concatenate([anchor_ref[...], anchor_ref[...]], axis=0)

    basis[0] = expand(force)
    for step in range(3):
        field = basis[step]
        edges = jnp.dot(field, pick_ref[...], preferred_element_type=jnp.float32, precision=HIGHEST_PREC)
        edge_send[step] = edges
        copies = [
            send(edge_send.at[step], edge_recv.at[step, d], edge_ssem.at[step, d], edge_rsem.at[step, d], device)
            for d, device in enumerate((on_row(1), on_row(-1), on_col(1), on_col(-1)))
        ]
        beside = (
            keep_left * pltpu.roll(field, 1, 1)
            + keep_right * pltpu.roll(field, nodes - 1, 1)
            + keep_up * pltpu.roll(field, MESH_X, 1)
            + keep_down * pltpu.roll(field, nodes - MESH_X, 1)
        )
        inner = stiff * (degree * field - beside) + anchor * field
        for copy in copies:
            copy.wait()
        partner = jnp.concatenate(
            [
                partners(*[
                    edge_recv[step, 0, c * tiles : (c + 1) * tiles],
                    edge_recv[step, 1, c * tiles : (c + 1) * tiles],
                    edges[c * tiles : (c + 1) * tiles],
                    edge_recv[step, 2, c * tiles : (c + 1) * tiles],
                    edge_recv[step, 3, c * tiles : (c + 1) * tiles],
                ])
                for c in range(2)
            ],
            axis=0,
        )
        gap = edges - partner
        pull = self_both * gap + link_both * pltpu.roll(gap, 127, 1) + pltpu.roll(link_both * gap, 1, 1)
        basis[step + 1] = inner + expand(pull)

    def total(k):
        product = basis[k // 2] * basis[(k + 1) // 2]
        return jnp.sum(jnp.sum(product, axis=0, keepdims=True), axis=1, keepdims=True)

    spots = lax.broadcasted_iota(jnp.int32, (8, 128), 1)
    sums = jnp.zeros((8, 128), jnp.float32)
    for k in range(6):
        sums = jnp.where(spots == k, total(k), sums)
    part[0] = sums
    copies = [
        send(part.at[0], part_row.at[by - 1], row_ssem.at[by - 1], row_rsem.at[by - 1], on_row(by))
        for by in range(1, rows)
    ]
    for by in range(1, rows):
        copies[by - 1].wait()
        sums = sums + part_row[by - 1]
    part[1] = sums
    copies = [
        send(part.at[1], part_col.at[by - 1], col_ssem.at[by - 1], col_rsem.at[by - 1], on_col(by))
        for by in range(1, cols)
    ]
    for by in range(1, cols):
        copies[by - 1].wait()
        sums = sums + part_col[by - 1]
    to_positions, to_residual = cg_weights([sums[0:1, k : k + 1] for k in range(6)])
    positions_ref[...] = sum(c * basis[i] for i, c in enumerate(to_positions))
    residual_ref[...] = sum(c * basis[i] for i, c in enumerate(to_residual))


def mesh_solve(terms, stiffness, anchor):
    rows, cols = lax.axis_size("row"), lax.axis_size("col")
    tiles, nodes = anchor.shape
    chosen = edge_selection()
    vmem = pl.BlockSpec(memory_space=pltpu.VMEM)
    dma = pltpu.SemaphoreType.DMA
    f32 = jnp.float32
    field = jax.ShapeDtypeStruct((2 * tiles, nodes), f32)

    def kernel(*refs):
        cg_kernel(rows, cols, *refs)

    return pl.pallas_call(
        kernel,
        out_shape=(field, field),
        in_specs=[vmem] * 5,
        out_specs=(vmem, vmem),
        scratch_shapes=[
            pltpu.VMEM((4, tiles, 128), f32),
            pltpu.VMEM((2, 4, tiles, 128), f32),
            pltpu.VMEM((3, 2 * tiles, 128), f32),
            pltpu.VMEM((3, 4, 2 * tiles, 128), f32),
            pltpu.VMEM((4, 2 * tiles, nodes), f32),
            pltpu.VMEM((2, 8, 128), f32),
            pltpu.VMEM((rows - 1, 8, 128), f32),
            pltpu.VMEM((cols - 1, 8, 128), f32),
            dma((2,)),
            dma((2,)),
            dma((3, 4)),
            dma((3, 4)),
            dma((rows - 1,)),
            dma((rows - 1,)),
            dma((cols - 1,)),
            dma((cols - 1,)),
        ],
        compiler_params=pltpu.CompilerParams(
            collective_id=0, has_side_effects=True, vmem_limit_bytes=32 * 1024 * 1024
        ),
    )(terms, stiffness, anchor, jnp.asarray(chosen), jnp.asarray(chosen.T))


def per_device(strips, pair_counts, pair_offsets, tile_stiffness, anchor):
    tile_count, patch_len = strips.shape[0], strips.shape[3]
    blocks = strips.shape[4] // patch_len
    table_list = tables()
    groups = tile_count // GROUP
    half = groups // 2
    east_a = passed_along(pack_left(strips, 0, half), "row", -1)
    east_b = passed_along(pack_left(strips, half, groups - half), "row", -1)
    next_top = passed_along(strips[0:1, 0, 1, :, :WIDE], "col", -1)
    south = unpack_sums(south_sums(strips, next_top, table_list))
    east = jnp.concatenate(
        [east_sums(strips, east_a, 0, table_list), east_sums(strips, east_b, half, table_list)], axis=0
    )
    east = unpack_sums(east)
    block_id = jnp.arange(blocks, dtype=jnp.int32)

    def terms(sums, counts, swap):
        weight, total = sums[:, 0], sums[:, 0] + SMALL_WEIGHT
        deep, along = sums[:, 1] / total, sums[:, 2] / total
        shifts = (along, deep) if swap else (deep, along)
        valid = block_id[None, None, :] < counts[:, None, None]
        return jnp.where(valid, jnp.stack((weight,) + shifts, axis=1), 0.0)

    east_terms = terms(east, pair_counts[:, 0, 0], False)
    south_terms = terms(south, pair_counts[:, 0, 1], True)
    match_terms = jnp.stack([east_terms, south_terms], axis=1)
    offsets = pair_offsets[:, 0].astype(jnp.float32)
    table = jnp.concatenate(
        [match_terms.reshape(tile_count, 6 * blocks), offsets, jnp.zeros((tile_count, 126 - 6 * blocks), jnp.float32)],
        axis=1,
    )
    positions, residual = mesh_solve(table, tile_stiffness, anchor[:, 0])
    nodes = MESH_Y * MESH_X

    def by_tile(field):
        return field.reshape(2, tile_count, nodes).transpose(1, 0, 2)[:, None]

    return match_terms[:, None], by_tile(positions), by_tile(residual)


def solution(mesh):
    return jax.shard_map(
        per_device,
        mesh=mesh,
        in_specs=(
            P("col", "row", None, None, None),
            P("col", "row", None),
            P("col", "row", None),
            P("col", "row"),
            P("col", "row", None),
        ),
        out_specs=(
            P("col", "row", None, None, None),
            P("col", "row", None, None),
            P("col", "row", None, None),
        ),
        check_vma=False,
    )
```

profile of v0, /device:TPU:0, one launch (start us, length us, event | category | flops | bytes accessed | tf_op | source)
XLA Modules:
  0.0 103.3 jit_solution(6644782953769452650)
XLA Ops:
  0.6 4.0 %copy-done = bf16[40,1,4,64,512]{4,3,2,1,0:T(8,128)(2,1)S(1)} copy-done((bf16[40,1,4,64,512]{4,3,2,1,0:T(8,128)(2,1)S(1)}, bf16[40,1,4,64,512]{4,3,2,1,0:T(8,128)(2,1)}, u32[]{:S(2)}) %copy-start) | copy-done | bytes 10485784
  5.2 1.3 %collective-permute-start = (bf16[10,64,640]{2,1,0:T(8,128)(2,1)S(1)}, bf16[10,64,640]{2,1,0:T(8,128)(2,1)S(1)}, u32[]{:S(2)}, u32[]{:S(2)}) collective-permute-start(bf16[10,64,640]{2,1,0:T(8,128)(2,1)S(1)} %shard_map.130), channel_id=1, source_target_pairs={{4,0},{8,4},{12,8},{16,12},{20,16},{24,20},{28,24},{5,1},{9,5},{13... | collective-permute-start | bytes 2457608 | tf_op jit(solution)/shard_map/ppermute | solution.py:190
  7.0 1.3 %collective-permute-start.1 = (bf16[10,64,640]{2,1,0:T(8,128)(2,1)S(1)}, bf16[10,64,640]{2,1,0:T(8,128)(2,1)S(1)}, u32[]{:S(2)}, u32[]{:S(2)}) collective-permute-start(bf16[10,64,640]{2,1,0:T(8,128)(2,1)S(1)} %shard_map.132), channel_id=1, source_target_pairs={{4,0},{8,4},{12,8},{16,12},{20,16},{24,20},{28,24},{5,1},{9,5},{13... | collective-permute-start | bytes 2457608 | tf_op jit(solution)/shard_map/ppermute | solution.py:190
  8.2 0.6 slice_bitcast_fusion
  8.9 1.3 %collective-permute-start.2 = (bf16[1,64,384]{2,1,0:T(8,128)(2,1)}, bf16[1,64,384]{2,1,0:T(8,128)(2,1)}, u32[]{:S(2)}, u32[]{:S(2)}) collective-permute-start(bf16[1,64,384]{2,1,0:T(8,128)(2,1)} %slice_bitcast_fusion), channel_id=1, source_target_pairs={{1,0},{2,1},{3,2},{5,4},{6,5},{7,6},{9,8},{10,9},{11,10},{13,12},{... | collective-permute-start | bytes 147464 | tf_op jit(solution)/shard_map/ppermute | solution.py:190
  10.2 0.6 iota_compare_fusion
  10.8 0.6 convert_bitcast_fusion
  11.3 1.4 %copy.36 = f32[40,2]{1,0:T(8,128)} copy(f32[40,2]{0,1:T(2,128)} %convert_bitcast_fusion) | data formatting | bytes 640 | tf_op jit(solution)/shard_map/convert_element_type | solution.py:459
  12.7 0.6 pad.16.clone
  13.3 0.6 pad.2.clone
  13.9 1.6 %copy.46 = f32[40,1,896]{2,0,1:T(8,128)} copy(f32[40,1,896]{2,1,0:T(1,128)} %param.15) | data formatting | bytes 286720
  15.5 1.3 %copy.37.refs_1_ = f32[40,1]{1,0:T(8,128)} copy(f32[40,1]{0,1:T(1,128)} %param.14) | data formatting | bytes 320 | tf_op args[3]
  16.8 4.0 %copy-done.1 = bf16[40,1,4,64,512]{4,3,2,1,0:T(8,128)(2,1)S(1)} copy-done((bf16[40,1,4,64,512]{4,3,2,1,0:T(8,128)(2,1)S(1)}, bf16[40,1,4,64,512]{4,3,2,1,0:T(8,128)(2,1)}, u32[]{:S(2)}) %copy-start.1) | copy-done | bytes 10485784
  20.8 0.8 copy-done.9
  21.6 11.8 %shard_map.134 = f32[10,10,128]{2,1,0:T(8,128)S(1)} custom-call(bf16[40,1,4,64,512]{4,3,2,1,0:T(8,128)(2,1)S(1)} %copy-done.1, bf16[40,1,4,64,512]{4,3,2,1,0:T(8,128)(2,1)S(1)} %copy-done.1, bf16[40,1,4,64,512]{4,3,2,1,0:T(8,128)(2,1)S(1)} %copy-done.1, bf16[1,64,384]{2,1,0:T(8,128)(2,1)} %collective-permute-done.2.next_ref, bf16[128,64]{1,0:T(8,128)(2,1)S(1)} %copy-done.9, ...), custom_call_target="tpu_custom_call" | custom-call | flops 3000000000 | bytes 4000000 | tf_op jit(solution)/shard_map/pallas_call | solution.py:154
  33.4 0.6 copy-done.8
  34.0 1.6 %copy.31 = f32[10,10,6]{0,2,1:T(8,128)} copy(f32[10,10,6]{2,1,0:T(8,128)} %bitcast.64) | data formatting | bytes 4800 | tf_op jit(solution)/shard_map/slice | solution.py:181
  35.6 1.4 %reshape.174 = f32[10,2,5,3,2]{0,4,3,2,1:T(2,128)} reshape(f32[10,10,6]{0,2,1:T(8,128)} %copy.31) | data formatting | bytes 4800 | tf_op jit(solution)/shard_map/reshape | solution.py:181
  37.0 1.4 %slice.68 = f32[10,2,4,3,2]{0,4,3,2,1:T(2,128)} slice(f32[10,2,5,3,2]{0,4,3,2,1:T(2,128)} %reshape.174), slice={[0:10], [0:2], [0:4], [0:3], [0:2]} | slice | bytes 3840 | tf_op jit(solution)/shard_map/slice | solution.py:182
  38.4 1.6 %copy.32 = f32[10,2,2,2,3,2]{2,1,0,5,3,4:T(2,128)} copy(f32[10,2,2,2,3,2]{0,5,4,3,2,1:T(2,128)} %bitcast.72) | data formatting | bytes 3840 | tf_op jit(solution)/shard_map/reshape | solution.py:182
  40.0 1.6 %reshape.176 = f32[40,3,4]{0,2,1:T(4,128)} reshape(f32[10,2,2,3,2,2]{2,1,0,5,4,3:T(2,128)} %bitcast.67) | data formatting | bytes 3840 | tf_op jit(solution)/shard_map/reshape | solution.py:182
  41.6 1.3 %slice_bitcast_fusion.1 = f32[10,2,2,3]{0,2,3,1:T(2,128)} fusion(f32[10,2,5,3,2]{0,4,3,2,1:T(2,128)} %reshape.174), kind=kLoop, calls=%fused_computation.11 | loop fusion | bytes 960 | tf_op jit(solution)/shard_map/transpose | solution.py:183
  42.9 1.4 %copy.33 = f32[10,2,2,3]{2,1,0,3:T(2,128)} copy(f32[10,2,2,3]{0,2,3,1:T(2,128)} %slice_bitcast_fusion.1) | data formatting | bytes 960 | tf_op jit(solution)/shard_map/transpose | solution.py:183
  44.3 1.4 %reshape.182 = f32[40,3,1]{0,2,1:T(1,128)} reshape(f32[10,2,2,3]{2,1,0,3:T(2,128)} %copy.33) | data formatting | bytes 960 | tf_op jit(solution)/shard_map/reshape | solution.py:183
  45.8 4.0 %copy-done.2 = bf16[40,1,4,64,512]{4,3,2,1,0:T(8,128)(2,1)S(1)} copy-done((bf16[40,1,4,64,512]{4,3,2,1,0:T(8,128)(2,1)S(1)}, bf16[40,1,4,64,512]{4,3,2,1,0:T(8,128)(2,1)}, u32[]{:S(2)}) %copy-start.2) | copy-done | bytes 10485784
  49.7 0.8 copy-done.10
  50.6 5.4 %shard_map.131 = f32[5,10,128]{2,1,0:T(8,128)S(1)} custom-call(bf16[40,1,4,64,512]{4,3,2,1,0:T(8,128)(2,1)S(1)} %copy-done.2, bf16[10,64,640]{2,1,0:T(8,128)(2,1)S(1)} %collective-permute-done.second_ref, bf16[128,64]{1,0:T(8,128)(2,1)S(1)} %copy-done.10, bf16[256,256]{1,0:T(8,128)(2,1)S(1)} %copy-done.4, bf16[256,256]{1,0:T(8,128)(2,1)S(1)} %copy-done.3, ...), custom_call_target="tpu_custom_call" | custom-call | flops 1500000000 | bytes 2000000 | tf_op jit(solution)/shard_map/pallas_call | solution.py:168
  56.0 5.4 %shard_map.133 = f32[5,10,128]{2,1,0:T(8,128)S(1)} custom-call(bf16[40,1,4,64,512]{4,3,2,1,0:T(8,128)(2,1)S(1)} %copy-done.2, bf16[10,64,640]{2,1,0:T(8,128)(2,1)S(1)} %collective-permute-done.1.second_ref, bf16[128,64]{1,0:T(8,128)(2,1)S(1)} %copy-done.10, bf16[256,256]{1,0:T(8,128)(2,1)S(1)} %copy-done.4, bf16[256,256]{1,0:T(8,128)(2,1)S(1)} %copy-done.3, ...), custom_call_target="tpu_custom_call" | custom-call | flops 1500000000 | bytes 2000000 | tf_op jit(solution)/shard_map/pallas_call | solution.py:168
  62.5 0.6 pad_maximum_fusion.1
  63.3 38.3 %shard_map.135 = (f32[80,896]{1,0:T(8,128)S(1)}, f32[80,896]{1,0:T(8,128)S(1)}) custom-call(f32[40,128]{1,0:T(8,128)S(1)} %maximum_maximum_fusion.refs_0_, f32[40,1]{1,0:T(8,128)S(1)} %copy-done.12, f32[40,896]{1,0:T(8,128)S(1)} %bitcast.63, f32[896,128]{1,0:T(8,128)S(1)} %copy-done.6, f32[128,896]{1,0:T(8,128)S(1)} %copy-done.7), custom_call_target="tpu_custom_call" | custom-call | tf_op jit(solution)/shard_map/pallas_call | solution.py:404
  101.6 0.9 copy.44
  102.4 0.9 copy.45
  (61 shorter events, 2.2 us)
Async XLA Ops:
  0.6 4.0 %copy-start = (bf16[40,1,4,64,512]{4,3,2,1,0:T(8,128)(2,1)S(1)}, bf16[40,1,4,64,512]{4,3,2,1,0:T(8,128)(2,1)}, u32[]{:S(2)}) copy-start(bf16[40,1,4,64,512]{4,3,2,1,0:T(8,128)(2,1)} %below_ref.1) | copy-start | bytes 31457284
  4.6 5.5 %copy-start.18 = (s32[40,1,2]{0,2,1:T(2,128)S(1)}, s32[40,1,2]{0,2,1:T(2,128)}, u32[]{:S(2)}) copy-start(s32[40,1,2]{0,2,1:T(2,128)} %param.12) | copy-start | bytes 964
  4.6 6.1 %copy-start.19 = (s32[40,1,2]{0,2,1:T(2,128)S(1)}, s32[40,1,2]{0,2,1:T(2,128)}, u32[]{:S(2)}) copy-start(s32[40,1,2]{0,2,1:T(2,128)} %param.13) | copy-start | bytes 964
  4.6 12.2 %copy-start.3 = (bf16[256,256]{1,0:T(8,128)(2,1)S(1)}, bf16[256,256]{1,0:T(8,128)(2,1)}, u32[]{:S(2)}) copy-start(bf16[256,256]{1,0:T(8,128)(2,1)} %constant.20.clone.bl_ref) | copy-start | bytes 393220
  4.6 12.2 %copy-start.4 = (bf16[256,256]{1,0:T(8,128)(2,1)S(1)}, bf16[256,256]{1,0:T(8,128)(2,1)}, u32[]{:S(2)}) copy-start(bf16[256,256]{1,0:T(8,128)(2,1)} %constant.7.clone.l_ref) | copy-start | bytes 393220
  4.6 12.2 %copy-start.11 = (bf16[64,128]{1,0:T(8,128)(2,1)S(1)}, bf16[64,128]{1,0:T(8,128)(2,1)}, u32[]{:S(2)}) copy-start(bf16[64,128]{1,0:T(8,128)(2,1)} %constant.21.clone.bd_ref) | copy-start | bytes 49156
  5.2 40.6 %collective-permute-start = (bf16[10,64,640]{2,1,0:T(8,128)(2,1)S(1)}, bf16[10,64,640]{2,1,0:T(8,128)(2,1)S(1)}, u32[]{:S(2)}, u32[]{:S(2)}) collective-permute-start(bf16[10,64,640]{2,1,0:T(8,128)(2,1)S(1)} %shard_map.130), channel_id=1, source_target_pairs={{4,0},{8,4},{12,8},{16,12},{20,16},{24,20},{28,24},{5,1},{9,5},{13... | collective-permute-start | bytes 2457608 | tf_op jit(solution)/shard_map/ppermute | solution.py:190
  7.0 49.1 %collective-permute-start.1 = (bf16[10,64,640]{2,1,0:T(8,128)(2,1)S(1)}, bf16[10,64,640]{2,1,0:T(8,128)(2,1)S(1)}, u32[]{:S(2)}, u32[]{:S(2)}) collective-permute-start(bf16[10,64,640]{2,1,0:T(8,128)(2,1)S(1)} %shard_map.132), channel_id=1, source_target_pairs={{4,0},{8,4},{12,8},{16,12},{20,16},{24,20},{28,24},{5,1},{9,5},{13... | collective-permute-start | bytes 2457608 | tf_op jit(solution)/shard_map/ppermute | solution.py:190
  8.9 7.9 %collective-permute-start.2 = (bf16[1,64,384]{2,1,0:T(8,128)(2,1)}, bf16[1,64,384]{2,1,0:T(8,128)(2,1)}, u32[]{:S(2)}, u32[]{:S(2)}) collective-permute-start(bf16[1,64,384]{2,1,0:T(8,128)(2,1)} %slice_bitcast_fusion), channel_id=1, source_target_pairs={{1,0},{2,1},{3,2},{5,4},{6,5},{7,6},{9,8},{10,9},{11,10},{13,12},{... | collective-permute-start | bytes 147464 | tf_op jit(solution)/shard_map/ppermute | solution.py:190
  16.8 4.0 %copy-start.1 = (bf16[40,1,4,64,512]{4,3,2,1,0:T(8,128)(2,1)S(1)}, bf16[40,1,4,64,512]{4,3,2,1,0:T(8,128)(2,1)}, u32[]{:S(2)}) copy-start(bf16[40,1,4,64,512]{4,3,2,1,0:T(8,128)(2,1)} %below_ref.1) | copy-start | bytes 31457284
  20.8 0.8 copy-start.9
  33.3 0.6 copy-start.8
  45.8 4.0 %copy-start.2 = (bf16[40,1,4,64,512]{4,3,2,1,0:T(8,128)(2,1)S(1)}, bf16[40,1,4,64,512]{4,3,2,1,0:T(8,128)(2,1)}, u32[]{:S(2)}) copy-start(bf16[40,1,4,64,512]{4,3,2,1,0:T(8,128)(2,1)} %below_ref.1) | copy-start | bytes 31457284
  49.7 0.8 copy-start.10
  50.5 11.8 %copy-start.14 = (f32[40,3,4]{0,2,1:T(4,128)S(1)}, f32[40,3,4]{0,2,1:T(4,128)}, u32[]{:S(2)}) copy-start(f32[40,3,4]{0,2,1:T(4,128)} %reshape.176) | copy-start | bytes 5764
  50.5 11.8 %copy-start.15 = (f32[40,3,1]{0,2,1:T(1,128)S(1)}, f32[40,3,1]{0,2,1:T(1,128)}, u32[]{:S(2)}) copy-start(f32[40,3,1]{0,2,1:T(1,128)} %reshape.182) | copy-start | bytes 1444
  50.5 11.8 %copy-start.21 = (f32[8]{0:T(128)S(1)}, f32[8]{0:T(128)}, u32[]{:S(2)}) copy-start(f32[8]{0:T(128)} %pad.16.clone) | copy-start | bytes 100
  50.5 11.9 %copy-start.17 = (pred[40,8]{0,1:T(8,128)(4,1)S(1)}, pred[40,8]{0,1:T(8,128)(4,1)}, u32[]{:S(2)}) copy-start(pred[40,8]{0,1:T(8,128)(4,1)} %get-tuple-element.23) | copy-start | bytes 964
  50.5 11.9 %copy-start.16 = (pred[40,8]{0,1:T(8,128)(4,1)S(1)}, pred[40,8]{0,1:T(8,128)(4,1)}, u32[]{:S(2)}) copy-start(pred[40,8]{0,1:T(8,128)(4,1)} %get-tuple-element.22) | copy-start | bytes 964
  50.5 12.6 %copy-start.13 = (f32[40,2]{1,0:T(8,128)S(1)}, f32[40,2]{1,0:T(8,128)}, u32[]{:S(2)}) copy-start(f32[40,2]{1,0:T(8,128)} %copy.36) | copy-start | bytes 964
  50.5 12.6 %copy-start.20 = (f32[128]{0:T(128)S(1)}, f32[128]{0:T(128)}, u32[]{:S(2)}) copy-start(f32[128]{0:T(128)} %pad.2.clone) | copy-start | bytes 1540
  50.5 12.7 %copy-start.5 = (f32[40,1,896]{2,0,1:T(8,128)S(1)}, f32[40,1,896]{2,0,1:T(8,128)}, u32[]{:S(2)}) copy-start(f32[40,1,896]{2,0,1:T(8,128)} %copy.46) | copy-start | bytes 430084
  50.6 12.7 %copy-start.6 = (f32[896,128]{1,0:T(8,128)S(1)}, f32[896,128]{1,0:T(8,128)}, u32[]{:S(2)}) copy-start(f32[896,128]{1,0:T(8,128)} %constant.22.clone.refs_3_) | copy-start | bytes 1376260
  50.6 12.7 %copy-start.12 = (f32[40,1]{1,0:T(8,128)S(1)}, f32[40,1]{1,0:T(8,128)}, u32[]{:S(2)}) copy-start(f32[40,1]{1,0:T(8,128)} %copy.37.refs_1_) | copy-start | bytes 484
  56.0 7.3 %copy-start.7 = (f32[128,896]{1,0:T(8,128)S(1)}, f32[128,896]{1,0:T(8,128)}, u32[]{:S(2)}) copy-start(f32[128,896]{1,0:T(8,128)} %constant.23.clone.refs_4_) | copy-start | bytes 1376260
where the time goes:
time: 104 us; the launch traced here: 103 us
  Pallas kernels  61.9 us (60%)
  local copies, waits for them, and re-layouts  34.6 us (33%)
  starting transfers between devices  3.84 us (4%)
  other arithmetic  1.94 us (2%)
    pallas_call x1, Pallas kernels, mesh_solve(): pl.pallas_call(kernel, out_shape=(field, field), in_specs=[vmem] * 5, out...  38.3 us
    unnamed x46, local copies, waits for them, and re-layouts  17.1 us
    pallas_call x1, Pallas kernels, south_sums(): pl.pallas_call(south_kernel, grid=(groups,), in_specs=[strip_spec(2), str...  11.8 us
    pallas_call x2, Pallas kernels, east_sums(): pl.pallas_call(east_kernel, grid=(groups,), in_specs=[strip_spec(3, start...  10.8 us
    ppermute x3, starting transfers between devices, passed_along(): return lax.ppermute(x, axis, pairs)  3.84 us
    reshape x4, local copies, waits for them, and re-layouts, unpack_sums(): sums[:, :, :4].reshape(groups, 2, 2, 2, 3, 2).transpose(0, 1, 2, 4, 3, 5)  3.7 us
    transpose x4, local copies, waits for them, and re-layouts, unpack_sums(): tail = sums[:, :, 4].transpose(0, 1, 3, 2).reshape(groups * 4, 3, 1)  2.83 us
  transfers between devices with their start and end apart: 3, of which 0 were waited for; matrix products, arithmetic and copies ran while one was open for 18% of the time, Pallas kernels for 17%

commit v1 on v0

--- a/solution.py
+++ b/solution.py
@@ -17,7 +17,6 @@
 PACKED = 2 * MOST * PATCH
 SMALL_WEIGHT = 1e-06
 NODE_GAP = 16.0
-HIGHEST_PREC = lax.Precision.HIGHEST
 
 
 def tables():
@@ -119,7 +118,7 @@
     ]
 
 
-PARAMS = pltpu.CompilerParams(vmem_limit_bytes=32 * 1024 * 1024)
+PARAMS = pltpu.CompilerParams(vmem_limit_bytes=50 * 1024 * 1024)
 
 
 def sums_shape(groups):
@@ -230,9 +229,20 @@
     return positions, residual
 
 
+def moved(values, table_ref):
+    size = values.shape[0]
+    high = values.astype(jnp.bfloat16)
+    rest = values - high.astype(jnp.float32)
+    middle = rest.astype(jnp.bfloat16)
+    low = (rest - middle.astype(jnp.float32)).astype(jnp.bfloat16)
+    parts = jnp.concatenate([high, middle, low], axis=0)
+    out = jnp.dot(parts, table_ref[...], preferred_element_type=jnp.float32)
+    return out[:size] + (out[size : 2 * size] + out[2 * size :])
+
+
 def cg_kernel(
     rows, cols, terms_ref, stiff_ref, anchor_ref, pick_ref, place_ref, positions_ref, residual_ref,
-    pair_send, pair_recv, edge_send, edge_recv, basis, part, part_row, part_col,
+    pair_send, pair_recv, edge_send, edge_recv, slab_send, slab_recv, basis, part, part_row, part_col,
     pair_ssem, pair_rsem, edge_ssem, edge_rsem, row_ssem, row_rsem, col_ssem, col_rsem,
 ):
     my_row, my_col = lax.axis_index("row"), lax.axis_index("col")
@@ -296,7 +306,7 @@
         copy.wait()
 
     def partners(west, east, own_part, north, south):
-        above = jnp.where(tile_id == 0, north[tiles - 1 : tiles], pltpu.roll(own_part, 1, 0))
+        above = jnp.where(tile_id == 0, north[-1:], pltpu.roll(own_part, 1, 0))
         low = pltpu.roll(jnp.where(group == 1, west, above), 96, 1)
         if east is None:
             return jnp.where(own, 0.0, low)
@@ -312,7 +322,7 @@
     force = jnp.concatenate([pair_send[2] - others[2], pair_send[3] - others[3]], axis=0)
 
     def expand(values):
-        return jnp.dot(values, place_ref[...], preferred_element_type=jnp.float32, precision=HIGHEST_PREC)
+        return moved(values, place_ref)
 
     nodes = MESH_Y * MESH_X
     spot = lax.broadcasted_iota(jnp.int32, (1, nodes), 1)
@@ -328,11 +338,17 @@
     basis[0] = expand(force)
     for step in range(3):
         field = basis[step]
-        edges = jnp.dot(field, pick_ref[...], preferred_element_type=jnp.float32, precision=HIGHEST_PREC)
+        edges = moved(field, pick_ref)
         edge_send[step] = edges
+        for c in range(2):
+            slab_send[step, 0, 8 * c : 8 * c + 8] = edges[(c + 1) * tiles - 8 : (c + 1) * tiles]
+            slab_send[step, 1, 8 * c : 8 * c + 8] = edges[c * tiles : c * tiles + 8]
         copies = [
-            send(edge_send.at[step], edge_recv.at[step, d], edge_ssem.at[step, d], edge_rsem.at[step, d], device)
-            for d, device in enumerate((on_row(1), on_row(-1), on_col(1), on_col(-1)))
+            send(edge_send.at[step], edge_recv.at[step, d], edge_ssem.at[step, d], edge_rsem.at[step, d], on_row(by))
+            for d, by in enumerate((1, -1))
+        ] + [
+            send(slab_send.at[step, d], slab_recv.at[step, d], edge_ssem.at[step, 2 + d], edge_rsem.at[step, 2 + d], on_col(by))
+            for d, by in enumerate((1, -1))
         ]
         beside = (
             keep_left * pltpu.roll(field, 1, 1)
@@ -349,8 +365,8 @@
                     edge_recv[step, 0, c * tiles : (c + 1) * tiles],
                     edge_recv[step, 1, c * tiles : (c + 1) * tiles],
                     edges[c * tiles : (c + 1) * tiles],
-                    edge_recv[step, 2, c * tiles : (c + 1) * tiles],
-                    edge_recv[step, 3, c * tiles : (c + 1) * tiles],
+                    slab_recv[step, 0, 8 * c : 8 * c + 8],
+                    slab_recv[step, 1, 8 * c : 8 * c + 8],
                 ])
                 for c in range(2)
             ],
@@ -410,7 +426,9 @@
             pltpu.VMEM((4, tiles, 128), f32),
             pltpu.VMEM((2, 4, tiles, 128), f32),
             pltpu.VMEM((3, 2 * tiles, 128), f32),
-            pltpu.VMEM((3, 4, 2 * tiles, 128), f32),
+            pltpu.VMEM((3, 2, 2 * tiles, 128), f32),
+            pltpu.VMEM((3, 2, 16, 128), f32),
+            pltpu.VMEM((3, 2, 16, 128), f32),
             pltpu.VMEM((4, 2 * tiles, nodes), f32),
             pltpu.VMEM((2, 8, 128), f32),
             pltpu.VMEM((rows - 1, 8, 128), f32),
@@ -425,9 +443,9 @@
             dma((cols - 1,)),
         ],
         compiler_params=pltpu.CompilerParams(
-            collective_id=0, has_side_effects=True, vmem_limit_bytes=32 * 1024 * 1024
+            collective_id=0, has_side_effects=True, vmem_limit_bytes=50 * 1024 * 1024
         ),
-    )(terms, stiffness, anchor, jnp.asarray(chosen), jnp.asarray(chosen.T))
+    )(terms, stiffness, anchor, jnp.asarray(chosen, jnp.bfloat16), jnp.asarray(chosen.T, jnp.bfloat16))
 
 
 def per_device(strips, pair_counts, pair_offsets, tile_stiffness, anchor):
@@ -435,14 +453,14 @@
     blocks = strips.shape[4] // patch_len
     table_list = tables()
     groups = tile_count // GROUP
-    half = groups // 2
+    half = groups - 2 * groups // 5
     east_a = passed_along(pack_left(strips, 0, half), "row", -1)
     east_b = passed_along(pack_left(strips, half, groups - half), "row", -1)
     next_top = passed_along(strips[0:1, 0, 1, :, :WIDE], "col", -1)
     south = unpack_sums(south_sums(strips, next_top, table_list))
-    east = jnp.concatenate(
-        [east_sums(strips, east_a, 0, table_list), east_sums(strips, east_b, half, table_list)], axis=0
-    )
+    sums_a = east_sums(strips, east_a, 0, table_list)
+    east_b, sums_a = lax.optimization_barrier((east_b, sums_a))
+    east = jnp.concatenate([sums_a, east_sums(strips, east_b, half, table_list)], axis=0)
     east = unpack_sums(east)
     block_id = jnp.arange(blocks, dtype=jnp.int32)
 

time: 104 us -> 98.3 us (0.945)
  local copies, waits for them, and re-layouts: 34.6 us -> 23.5 us
  Pallas kernels: 61.9 us -> 66.9 us
    unnamed x46 -> x40, local copies, waits for them, and re-layouts: 17.1 us -> 5.15 us
    pallas_call x2, Pallas kernels: 1.03 us -> 5.43 us  [pack_left(): pl.pallas_call(pack_kernel, grid=(groups,), in_specs=[strip_spec(0, start...]
    pallas_call x2, Pallas kernels: 10.8 us -> 12.5 us  [east_sums(): pl.pallas_call(east_kernel, grid=(groups,), in_specs=[strip_spec(3, start...]
  transfers between devices with their start and end apart: 3 -> 3, of which waited for: 0 -> 0; matrix products, arithmetic and copies ran while one was open for 18% -> 20% of each run, Pallas kernels for 17% -> 22%
where the time goes in v1:
time: 98.3 us; the launch traced here: 97.2 us
  Pallas kernels  66.9 us (68%)
  local copies, waits for them, and re-layouts  23.5 us (24%)
  starting transfers between devices  3.86 us (4%)
  other arithmetic  1.95 us (2%)
    pallas_call x1, Pallas kernels, mesh_solve(): pl.pallas_call(kernel, out_shape=(field, field), in_specs=[vmem] * 5, out...  37.3 us
    pallas_call x2, Pallas kernels, east_sums(): pl.pallas_call(east_kernel, grid=(groups,), in_specs=[strip_spec(3, start...  12.5 us
    pallas_call x1, Pallas kernels, south_sums(): pl.pallas_call(south_kernel, grid=(groups,), in_specs=[strip_spec(2), str...  11.7 us
    pallas_call x2, Pallas kernels, pack_left(): pl.pallas_call(pack_kernel, grid=(groups,), in_specs=[strip_spec(0, start...  5.43 us
    unnamed x40, local copies, waits for them, and re-layouts  5.15 us
    ppermute x3, starting transfers between devices, passed_along(): return lax.ppermute(x, axis, pairs)  3.86 us
    reshape x4, local copies, waits for them, and re-layouts, unpack_sums(): sums[:, :, :4].reshape(groups, 2, 2, 2, 3, 2).transpose(0, 1, 2, 4, 3, 5)  3.71 us
    transpose x4, local copies, waits for them, and re-layouts, unpack_sums(): tail = sums[:, :, 4].transpose(0, 1, 3, 2).reshape(groups * 4, 3, 1)  2.83 us
  transfers between devices with their start and end apart: 3, of which 0 were waited for; matrix products, arithmetic and copies ran while one was open for 20% of the time, Pallas kernels for 22%

profile of v1, /device:TPU:0, one launch (start us, length us, event | category | flops | bytes accessed | tf_op | source)
XLA Modules:
  0.0 97.2 jit_solution(7929498305357031455)
XLA Ops:
  0.7 3.3 %shard_map.131 = bf16[12,64,640]{2,1,0:T(8,128)(2,1)S(1)} custom-call(bf16[40,1,4,64,512]{4,3,2,1,0:T(8,128)(2,1)} %below_ref.1), custom_call_target="tpu_custom_call" | custom-call | tf_op jit(solution)/shard_map/pallas_call | solution.py:136
  4.0 1.3 %collective-permute-start.1 = (bf16[12,64,640]{2,1,0:T(8,128)(2,1)S(1)}, bf16[12,64,640]{2,1,0:T(8,128)(2,1)S(1)}, u32[]{:S(2)}, u32[]{:S(2)}) collective-permute-start(bf16[12,64,640]{2,1,0:T(8,128)(2,1)S(1)} %shard_map.131), channel_id=1, source_target_pairs={{4,0},{8,4},{12,8},{16,12},{20,16},{24,20},{28,24},{5,1},{9,5},{13... | collective-permute-start | bytes 2949128 | tf_op jit(solution)/shard_map/ppermute | solution.py:189
  5.3 2.2 %shard_map.130 = bf16[8,64,640]{2,1,0:T(8,128)(2,1)S(1)} custom-call(bf16[40,1,4,64,512]{4,3,2,1,0:T(8,128)(2,1)} %below_ref.1), custom_call_target="tpu_custom_call" | custom-call | tf_op jit(solution)/shard_map/pallas_call | solution.py:136
  7.4 1.3 %collective-permute-start = (bf16[8,64,640]{2,1,0:T(8,128)(2,1)S(1)}, bf16[8,64,640]{2,1,0:T(8,128)(2,1)S(1)}, u32[]{:S(2)}, u32[]{:S(2)}) collective-permute-start(bf16[8,64,640]{2,1,0:T(8,128)(2,1)S(1)} %shard_map.130), channel_id=1, source_target_pairs={{4,0},{8,4},{12,8},{16,12},{20,16},{24,20},{28,24},{5,1},{9,5},{13... | collective-permute-start | bytes 1966088 | tf_op jit(solution)/shard_map/ppermute | solution.py:189
  8.7 1.4 %slice_bitcast_fusion = bf16[1,64,384]{2,1,0:T(8,128)(2,1)} fusion(bf16[40,1,4,64,512]{4,3,2,1,0:T(8,128)(2,1)} %below_ref.1), kind=kLoop, calls=%fused_computation.4 | loop fusion | bytes 98304 | tf_op jit(solution)/shard_map/squeeze | solution.py:459
  10.2 1.3 %collective-permute-start.2 = (bf16[1,64,384]{2,1,0:T(8,128)(2,1)}, bf16[1,64,384]{2,1,0:T(8,128)(2,1)}, u32[]{:S(2)}, u32[]{:S(2)}) collective-permute-start(bf16[1,64,384]{2,1,0:T(8,128)(2,1)} %slice_bitcast_fusion), channel_id=1, source_target_pairs={{1,0},{2,1},{3,2},{5,4},{6,5},{7,6},{9,8},{10,9},{11,10},{13,12},{... | collective-permute-start | bytes 147464 | tf_op jit(solution)/shard_map/ppermute | solution.py:189
  11.5 0.6 iota_compare_fusion
  12.1 0.6 convert_bitcast_fusion
  12.6 1.4 %copy.36 = f32[40,2]{1,0:T(8,128)} copy(f32[40,2]{0,1:T(2,128)} %convert_bitcast_fusion) | data formatting | bytes 640 | tf_op jit(solution)/shard_map/convert_element_type | solution.py:477
  14.0 0.6 pad.16.clone
  14.6 0.6 pad.2.clone
  15.2 1.6 %copy.46 = f32[40,1,896]{2,0,1:T(8,128)} copy(f32[40,1,896]{2,1,0:T(1,128)} %param.15) | data formatting | bytes 286720
  16.7 1.4 %copy.37.refs_1_ = f32[40,1]{1,0:T(8,128)} copy(f32[40,1]{0,1:T(1,128)} %param.14) | data formatting | bytes 320 | tf_op args[3]
  18.1 0.7 copy-done.4
  18.9 11.7 %shard_map.134 = f32[10,10,128]{2,1,0:T(8,128)S(1)} custom-call(bf16[40,1,4,64,512]{4,3,2,1,0:T(8,128)(2,1)} %below_ref.1, bf16[40,1,4,64,512]{4,3,2,1,0:T(8,128)(2,1)} %below_ref.1, bf16[40,1,4,64,512]{4,3,2,1,0:T(8,128)(2,1)} %below_ref.1, bf16[1,64,384]{2,1,0:T(8,128)(2,1)} %collective-permute-done.2.next_ref, bf16[128,64]{1,0:T(8,128)(2,1)S(1)} %copy-done.4, ...), custom_call_target="tpu_custom_call" | custom-call | flops 3000000000 | bytes 4000000 | tf_op jit(solution)/shard_map/pallas_call | solution.py:153
  30.6 0.6 copy-done.3
  31.2 1.6 %copy.31 = f32[10,10,6]{0,2,1:T(8,128)} copy(f32[10,10,6]{2,1,0:T(8,128)} %bitcast.64) | data formatting | bytes 4800 | tf_op jit(solution)/shard_map/slice | solution.py:180
  32.8 1.4 %reshape.174 = f32[10,2,5,3,2]{0,4,3,2,1:T(2,128)} reshape(f32[10,10,6]{0,2,1:T(8,128)} %copy.31) | data formatting | bytes 4800 | tf_op jit(solution)/shard_map/reshape | solution.py:180
  34.2 1.4 %slice.68 = f32[10,2,4,3,2]{0,4,3,2,1:T(2,128)} slice(f32[10,2,5,3,2]{0,4,3,2,1:T(2,128)} %reshape.174), slice={[0:10], [0:2], [0:4], [0:3], [0:2]} | slice | bytes 3840 | tf_op jit(solution)/shard_map/slice | solution.py:181
  35.6 1.6 %copy.32 = f32[10,2,2,2,3,2]{2,1,0,5,3,4:T(2,128)} copy(f32[10,2,2,2,3,2]{0,5,4,3,2,1:T(2,128)} %bitcast.72) | data formatting | bytes 3840 | tf_op jit(solution)/shard_map/reshape | solution.py:181
  37.2 1.7 %reshape.176 = f32[40,3,4]{0,2,1:T(4,128)} reshape(f32[10,2,2,3,2,2]{2,1,0,5,4,3:T(2,128)} %bitcast.67) | data formatting | bytes 3840 | tf_op jit(solution)/shard_map/reshape | solution.py:181
  38.8 1.3 %slice_bitcast_fusion.1 = f32[10,2,2,3]{0,2,3,1:T(2,128)} fusion(f32[10,2,5,3,2]{0,4,3,2,1:T(2,128)} %reshape.174), kind=kLoop, calls=%fused_computation.11 | loop fusion | bytes 960 | tf_op jit(solution)/shard_map/transpose | solution.py:182
  40.1 1.4 %copy.33 = f32[10,2,2,3]{2,1,0,3:T(2,128)} copy(f32[10,2,2,3]{0,2,3,1:T(2,128)} %slice_bitcast_fusion.1) | data formatting | bytes 960 | tf_op jit(solution)/shard_map/transpose | solution.py:182
  41.5 1.4 %reshape.182 = f32[40,3,1]{0,2,1:T(1,128)} reshape(f32[10,2,2,3]{2,1,0,3:T(2,128)} %copy.33) | data formatting | bytes 960 | tf_op jit(solution)/shard_map/reshape | solution.py:182
  43.0 0.8 copy-done.5
  43.8 7.4 %shard_map.132 = f32[6,10,128]{2,1,0:T(8,128)S(1)} custom-call(bf16[40,1,4,64,512]{4,3,2,1,0:T(8,128)(2,1)} %below_ref.1, bf16[12,64,640]{2,1,0:T(8,128)(2,1)S(1)} %collective-permute-done.1.second_ref, bf16[128,64]{1,0:T(8,128)(2,1)S(1)} %copy-done.5, bf16[256,256]{1,0:T(8,128)(2,1)S(1)} %copy-done.1, bf16[256,256]{1,0:T(8,128)(2,1)S(1)} %copy-done, ...), custom_call_target="tpu_custom_call" | custom-call | flops 1800000000 | bytes 2400000 | tf_op jit(solution)/shard_map/pallas_call | solution.py:167
  51.2 5.2 %shard_map.133 = f32[4,10,128]{2,1,0:T(8,128)S(1)} custom-call(bf16[40,1,4,64,512]{4,3,2,1,0:T(8,128)(2,1)} %below_ref.1, bf16[8,64,640]{2,1,0:T(8,128)(2,1)S(1)} %collective-permute-done.second_ref, bf16[128,64]{1,0:T(8,128)(2,1)S(1)} %copy-done.5, bf16[256,256]{1,0:T(8,128)(2,1)S(1)} %copy-done.1, bf16[256,256]{1,0:T(8,128)(2,1)S(1)} %copy-done, ...), custom_call_target="tpu_custom_call" | custom-call | flops 1200000000 | bytes 1600000 | tf_op jit(solution)/shard_map/pallas_call | solution.py:167
  56.6 0.3 copy.28
  57.4 0.6 pad_maximum_fusion.1
  58.2 37.3 %shard_map.135 = (f32[80,896]{1,0:T(8,128)S(1)}, f32[80,896]{1,0:T(8,128)S(1)}) custom-call(f32[40,128]{1,0:T(8,128)S(1)} %maximum_maximum_fusion.refs_0_, f32[40,1]{1,0:T(8,128)S(1)} %copy-done.9, f32[40,896]{1,0:T(8,128)S(1)} %bitcast.63, bf16[896,128]{1,0:T(8,128)(2,1)S(1)} %copy-done.6, bf16[128,896]{1,0:T(8,128)(2,1)S(1)} %copy-done.7), custom_call_target="tpu_custom_call" | custom-call | tf_op jit(solution)/shard_map/pallas_call | solution.py:420
  95.5 0.9 copy.44
  96.4 0.9 copy.45
  (55 shorter events, 0.9 us)
Async XLA Ops:
  0.6 17.5 %copy-start = (bf16[256,256]{1,0:T(8,128)(2,1)S(1)}, bf16[256,256]{1,0:T(8,128)(2,1)}, u32[]{:S(2)}) copy-start(bf16[256,256]{1,0:T(8,128)(2,1)} %constant.20.clone.bl_ref) | copy-start | bytes 393220
  0.6 17.5 %copy-start.1 = (bf16[256,256]{1,0:T(8,128)(2,1)S(1)}, bf16[256,256]{1,0:T(8,128)(2,1)}, u32[]{:S(2)}) copy-start(bf16[256,256]{1,0:T(8,128)(2,1)} %constant.7.clone.l_ref) | copy-start | bytes 393220
  0.7 17.4 %copy-start.8 = (bf16[64,128]{1,0:T(8,128)(2,1)S(1)}, bf16[64,128]{1,0:T(8,128)(2,1)}, u32[]{:S(2)}) copy-start(bf16[64,128]{1,0:T(8,128)(2,1)} %constant.21.clone.bd_ref) | copy-start | bytes 49156
  0.7 10.8 %copy-start.15 = (s32[40,1,2]{0,2,1:T(2,128)S(1)}, s32[40,1,2]{0,2,1:T(2,128)}, u32[]{:S(2)}) copy-start(s32[40,1,2]{0,2,1:T(2,128)} %param.12) | copy-start | bytes 964
  0.7 11.4 %copy-start.16 = (s32[40,1,2]{0,2,1:T(2,128)S(1)}, s32[40,1,2]{0,2,1:T(2,128)}, u32[]{:S(2)}) copy-start(s32[40,1,2]{0,2,1:T(2,128)} %param.13) | copy-start | bytes 964
  4.0 39.0 %collective-permute-start.1 = (bf16[12,64,640]{2,1,0:T(8,128)(2,1)S(1)}, bf16[12,64,640]{2,1,0:T(8,128)(2,1)S(1)}, u32[]{:S(2)}, u32[]{:S(2)}) collective-permute-start(bf16[12,64,640]{2,1,0:T(8,128)(2,1)S(1)} %shard_map.131), channel_id=1, source_target_pairs={{4,0},{8,4},{12,8},{16,12},{20,16},{24,20},{28,24},{5,1},{9,5},{13... | collective-permute-start | bytes 2949128 | tf_op jit(solution)/shard_map/ppermute | solution.py:189
  7.4 43.8 %collective-permute-start = (bf16[8,64,640]{2,1,0:T(8,128)(2,1)S(1)}, bf16[8,64,640]{2,1,0:T(8,128)(2,1)S(1)}, u32[]{:S(2)}, u32[]{:S(2)}) collective-permute-start(bf16[8,64,640]{2,1,0:T(8,128)(2,1)S(1)} %shard_map.130), channel_id=1, source_target_pairs={{4,0},{8,4},{12,8},{16,12},{20,16},{24,20},{28,24},{5,1},{9,5},{13... | collective-permute-start | bytes 1966088 | tf_op jit(solution)/shard_map/ppermute | solution.py:189
  10.2 7.9 %collective-permute-start.2 = (bf16[1,64,384]{2,1,0:T(8,128)(2,1)}, bf16[1,64,384]{2,1,0:T(8,128)(2,1)}, u32[]{:S(2)}, u32[]{:S(2)}) collective-permute-start(bf16[1,64,384]{2,1,0:T(8,128)(2,1)} %slice_bitcast_fusion), channel_id=1, source_target_pairs={{1,0},{2,1},{3,2},{5,4},{6,5},{7,6},{9,8},{10,9},{11,10},{13,12},{... | collective-permute-start | bytes 147464 | tf_op jit(solution)/shard_map/ppermute | solution.py:189
  18.1 0.8 copy-start.4
  30.5 0.6 copy-start.3
  43.0 0.8 copy-start.5
  43.7 13.5 %copy-start.11 = (f32[40,3,4]{0,2,1:T(4,128)S(1)}, f32[40,3,4]{0,2,1:T(4,128)}, u32[]{:S(2)}) copy-start(f32[40,3,4]{0,2,1:T(4,128)} %reshape.176) | copy-start | bytes 5764
  43.7 13.5 %copy-start.12 = (f32[40,3,1]{0,2,1:T(1,128)S(1)}, f32[40,3,1]{0,2,1:T(1,128)}, u32[]{:S(2)}) copy-start(f32[40,3,1]{0,2,1:T(1,128)} %reshape.182) | copy-start | bytes 1444
  43.7 13.5 %copy-start.18 = (f32[8]{0:T(128)S(1)}, f32[8]{0:T(128)}, u32[]{:S(2)}) copy-start(f32[8]{0:T(128)} %pad.16.clone) | copy-start | bytes 100
  43.7 13.6 %copy-start.14 = (pred[40,8]{0,1:T(8,128)(4,1)S(1)}, pred[40,8]{0,1:T(8,128)(4,1)}, u32[]{:S(2)}) copy-start(pred[40,8]{0,1:T(8,128)(4,1)} %get-tuple-element.27) | copy-start | bytes 964
  43.7 13.6 %copy-start.13 = (pred[40,8]{0,1:T(8,128)(4,1)S(1)}, pred[40,8]{0,1:T(8,128)(4,1)}, u32[]{:S(2)}) copy-start(pred[40,8]{0,1:T(8,128)(4,1)} %get-tuple-element.26) | copy-start | bytes 964
  43.7 14.3 %copy-start.10 = (f32[40,2]{1,0:T(8,128)S(1)}, f32[40,2]{1,0:T(8,128)}, u32[]{:S(2)}) copy-start(f32[40,2]{1,0:T(8,128)} %copy.36) | copy-start | bytes 964
  43.8 14.3 %copy-start.17 = (f32[128]{0:T(128)S(1)}, f32[128]{0:T(128)}, u32[]{:S(2)}) copy-start(f32[128]{0:T(128)} %pad.2.clone) | copy-start | bytes 1540
  43.8 14.4 %copy-start.2 = (f32[40,1,896]{2,0,1:T(8,128)S(1)}, f32[40,1,896]{2,0,1:T(8,128)}, u32[]{:S(2)}) copy-start(f32[40,1,896]{2,0,1:T(8,128)} %copy.46) | copy-start | bytes 430084
  43.8 14.4 %copy-start.6 = (bf16[896,128]{1,0:T(8,128)(2,1)S(1)}, bf16[896,128]{1,0:T(8,128)(2,1)}, u32[]{:S(2)}) copy-start(bf16[896,128]{1,0:T(8,128)(2,1)} %constant.22.clone.refs_3_) | copy-start | bytes 688132
  43.8 14.4 %copy-start.7 = (bf16[128,896]{1,0:T(8,128)(2,1)S(1)}, bf16[128,896]{1,0:T(8,128)(2,1)}, u32[]{:S(2)}) copy-start(bf16[128,896]{1,0:T(8,128)(2,1)} %constant.23.clone.refs_4_) | copy-start | bytes 688132
  43.8 14.4 %copy-start.9 = (f32[40,1]{1,0:T(8,128)S(1)}, f32[40,1]{1,0:T(8,128)}, u32[]{:S(2)}) copy-start(f32[40,1]{1,0:T(8,128)} %copy.37.refs_1_) | copy-start | bytes 484

commit v2 on v1

--- a/solution.py
+++ b/solution.py
@@ -242,7 +242,7 @@
 
 def cg_kernel(
     rows, cols, terms_ref, stiff_ref, anchor_ref, pick_ref, place_ref, positions_ref, residual_ref,
-    pair_send, pair_recv, edge_send, edge_recv, slab_send, slab_recv, basis, part, part_row, part_col,
+    pair_send, below_send, pair_recv, below_recv, edge_send, edge_recv, slab_send, slab_recv, basis, part, part_row, part_col,
     pair_ssem, pair_rsem, edge_ssem, edge_rsem, row_ssem, row_rsem, col_ssem, col_rsem,
 ):
     my_row, my_col = lax.axis_index("row"), lax.axis_index("col")
@@ -293,33 +293,41 @@
         link_term += weighted * after
         force_x += weighted * term(8 + k)
         force_y += weighted * term(16 + k)
-    pair_send[0] = jnp.where(inside, self_term, 0.0)
-    pair_send[1] = jnp.where(linked, link_term, 0.0)
-    pair_send[2] = jnp.where(inside, force_x, 0.0)
-    pair_send[3] = jnp.where(inside, force_y, 0.0)
+    quantities = [
+        jnp.where(inside, self_term, 0.0),
+        jnp.where(linked, link_term, 0.0),
+        jnp.where(inside, force_x, 0.0),
+        jnp.where(inside, force_y, 0.0),
+    ]
+
+    def turned(values, by):
+        return pltpu.roll(values, by % 128, 1) if by % 128 else values
+
+    def by_group(choices):
+        out = choices[0]
+        for g in range(1, 4):
+            out = jnp.where(group == g, choices[g], out)
+        return out
+
+    pair_send[...] = by_group([turned(q, 32 * c - 32) for c, q in enumerate(quantities)])
+    below_send[...] = by_group([turned(q, 32 * c - 96) for c, q in enumerate(quantities)])[tiles - 8 :]
     pl.semaphore_wait(barrier, rows + cols - 2)
     copies = [
-        send(pair_send, pair_recv.at[0], pair_ssem.at[0], pair_rsem.at[0], on_row(1)),
-        send(pair_send, pair_recv.at[1], pair_ssem.at[1], pair_rsem.at[1], on_col(1)),
+        send(pair_send, pair_recv, pair_ssem.at[0], pair_rsem.at[0], on_row(1)),
+        send(below_send, below_recv, pair_ssem.at[1], pair_rsem.at[1], on_col(1)),
     ]
     for copy in copies:
         copy.wait()
-
-    def partners(west, east, own_part, north, south):
-        above = jnp.where(tile_id == 0, north[-1:], pltpu.roll(own_part, 1, 0))
-        low = pltpu.roll(jnp.where(group == 1, west, above), 96, 1)
-        if east is None:
-            return jnp.where(own, 0.0, low)
-        below = jnp.where(tile_id == tiles - 1, south[0:1], pltpu.roll(own_part, tiles - 1, 0))
-        high = pltpu.roll(jnp.where(group == 0, east, below), 32, 1)
-        return jnp.where(own, high, low)
-
-    others = [partners(pair_recv[0, c], None, pair_send[c], pair_recv[1, c], None) for c in range(4)]
-    self_term = pair_send[0] + others[0]
-    link_term = pair_send[1] + others[1]
+    others = []
+    for c, q in enumerate(quantities):
+        first = turned(below_recv[...], 64 - 32 * c)[7:8]
+        above = jnp.where(tile_id == 0, first, turned(pltpu.roll(q, 1, 0), -32))
+        others.append(by_group([turned(pair_recv[...], -32 * c), zero, above, zero]))
+    self_term = quantities[0] + others[0]
+    link_term = quantities[1] + others[1]
     self_both = jnp.concatenate([self_term, self_term], axis=0)
     link_both = jnp.concatenate([link_term, link_term], axis=0)
-    force = jnp.concatenate([pair_send[2] - others[2], pair_send[3] - others[3]], axis=0)
+    force = jnp.concatenate([quantities[2] - others[2], quantities[3] - others[3]], axis=0)
 
     def expand(values):
         return moved(values, place_ref)
@@ -339,12 +347,14 @@
     for step in range(3):
         field = basis[step]
         edges = moved(field, pick_ref)
-        edge_send[step] = edges
+        split = [edges[:tiles], edges[tiles:]]
+        edge_send[step, 0] = jnp.where(group == 0, turned(split[0], -32), split[1])
+        edge_send[step, 1] = jnp.where(group == 0, split[0], turned(split[1], 32))
         for c in range(2):
             slab_send[step, 0, 8 * c : 8 * c + 8] = edges[(c + 1) * tiles - 8 : (c + 1) * tiles]
             slab_send[step, 1, 8 * c : 8 * c + 8] = edges[c * tiles : c * tiles + 8]
         copies = [
-            send(edge_send.at[step], edge_recv.at[step, d], edge_ssem.at[step, d], edge_rsem.at[step, d], on_row(by))
+            send(edge_send.at[step, d], edge_recv.at[step, d], edge_ssem.at[step, d], edge_rsem.at[step, d], on_row(by))
             for d, by in enumerate((1, -1))
         ] + [
             send(slab_send.at[step, d], slab_recv.at[step, d], edge_ssem.at[step, 2 + d], edge_rsem.at[step, 2 + d], on_col(by))
@@ -359,19 +369,16 @@
         inner = stiff * (degree * field - beside) + anchor * field
         for copy in copies:
             copy.wait()
-        partner = jnp.concatenate(
-            [
-                partners(*[
-                    edge_recv[step, 0, c * tiles : (c + 1) * tiles],
-                    edge_recv[step, 1, c * tiles : (c + 1) * tiles],
-                    edges[c * tiles : (c + 1) * tiles],
-                    slab_recv[step, 0, 8 * c : 8 * c + 8],
-                    slab_recv[step, 1, 8 * c : 8 * c + 8],
-                ])
-                for c in range(2)
-            ],
-            axis=0,
-        )
+        partner = []
+        for c in range(2):
+            north = slab_recv[step, 0, 8 * c + 7 : 8 * c + 8]
+            south = slab_recv[step, 1, 8 * c : 8 * c + 1]
+            above = jnp.where(tile_id == 0, north, pltpu.roll(split[c], 1, 0))
+            below = jnp.where(tile_id == tiles - 1, south, pltpu.roll(split[c], tiles - 1, 0))
+            west = turned(edge_recv[step, 0], -32 * c)
+            east = turned(edge_recv[step, 1], 32 - 32 * c)
+            partner.append(by_group([west, east, turned(above, -32), turned(below, 32)]))
+        partner = jnp.concatenate(partner, axis=0)
         gap = edges - partner
         pull = self_both * gap + link_both * pltpu.roll(gap, 127, 1) + pltpu.roll(link_both * gap, 1, 1)
         basis[step + 1] = inner + expand(pull)
@@ -423,10 +430,12 @@
         in_specs=[vmem] * 5,
         out_specs=(vmem, vmem),
         scratch_shapes=[
-            pltpu.VMEM((4, tiles, 128), f32),
-            pltpu.VMEM((2, 4, tiles, 128), f32),
-            pltpu.VMEM((3, 2 * tiles, 128), f32),
-            pltpu.VMEM((3, 2, 2 * tiles, 128), f32),
+            pltpu.VMEM((tiles, 128), f32),
+            pltpu.VMEM((8, 128), f32),
+            pltpu.VMEM((tiles, 128), f32),
+            pltpu.VMEM((8, 128), f32),
+            pltpu.VMEM((3, 2, tiles, 128), f32),
+            pltpu.VMEM((3, 2, tiles, 128), f32),
             pltpu.VMEM((3, 2, 16, 128), f32),
             pltpu.VMEM((3, 2, 16, 128), f32),
             pltpu.VMEM((4, 2 * tiles, nodes), f32),
@@ -457,11 +466,12 @@
     east_a = passed_along(pack_left(strips, 0, half), "row", -1)
     east_b = passed_along(pack_left(strips, half, groups - half), "row", -1)
     next_top = passed_along(strips[0:1, 0, 1, :, :WIDE], "col", -1)
-    south = unpack_sums(south_sums(strips, next_top, table_list))
+    south = south_sums(strips, next_top, table_list)
     sums_a = east_sums(strips, east_a, 0, table_list)
     east_b, sums_a = lax.optimization_barrier((east_b, sums_a))
-    east = jnp.concatenate([sums_a, east_sums(strips, east_b, half, table_list)], axis=0)
-    east = unpack_sums(east)
+    sums_b = east_sums(strips, east_b, half, table_list)
+    sums = unpack_sums(jnp.concatenate([sums_a, sums_b, south], axis=0))
+    east, south = sums[:tile_count], sums[tile_count:]
     block_id = jnp.arange(blocks, dtype=jnp.int32)
 
     def terms(sums, counts, swap):

time: 98.3 us -> 85 us (0.86)
  local copies, waits for them, and re-layouts: 23.5 us -> 10.6 us
  Pallas kernels: 66.9 us -> 60.5 us
  waiting for transfers between devices: 0.01 us -> 5.97 us
    pallas_call x1, Pallas kernels: 37.3 us -> 30.9 us  [mesh_solve(): pl.pallas_call(kernel, out_shape=(field, field), in_specs=[vmem] * 5, out...]
    ppermute x3, waiting for transfers between devices: 0.01 us -> 5.97 us  [passed_along(): return lax.ppermute(x, axis, pairs)]
    reshape x4 -> x2, local copies, waits for them, and re-layouts: 3.71 us -> 0.57 us  [unpack_sums(): sums[:, :, :4].reshape(groups, 2, 2, 2, 3, 2).transpose(0, 1, 2, 4, 3, 5)]
    transpose x4 -> x2, local copies, waits for them, and re-layouts: 2.83 us -> 0.13 us  [unpack_sums(): tail = sums[:, :, 4].transpose(0, 1, 3, 2).reshape(groups * 4, 3, 1)]
    slice x2 -> x1, local copies, waits for them, and re-layouts: 1.77 us -> 0.15 us  [unpack_sums(): sums = sums[:, :, :6].reshape(groups, 2, MOST, 3, 2)]
    unnamed x40 -> x32, local copies, waits for them, and re-layouts: 5.15 us -> 3.74 us
    reshape x2 -> x1, local copies, waits for them, and re-layouts: 1.42 us -> 0.02 us  [unpack_sums(): sums = sums[:, :, :6].reshape(groups, 2, MOST, 3, 2)]
    reshape x2 -> x1, local copies, waits for them, and re-layouts: 1.52 us -> 0.13 us  [unpack_sums(): tail = sums[:, :, 4].transpose(0, 1, 3, 2).reshape(groups * 4, 3, 1)]
  transfers between devices with their start and end apart: 3 -> 3, of which waited for: 0 -> 2; matrix products, arithmetic and copies ran while one was open for 20% -> 10% of each run, Pallas kernels for 22% -> 25%
where the time goes in v2:
time: 85 us; the launch traced here: 84.4 us
  Pallas kernels  60.5 us (71%)
  local copies, waits for them, and re-layouts  10.6 us (12%)
  waiting for transfers between devices  5.97 us (7%)
  starting transfers between devices  3.86 us (5%)
  other arithmetic  2.57 us (3%)
  between operations  0.9 us (1%)
    pallas_call x1, Pallas kernels, mesh_solve(): pl.pallas_call(kernel, out_shape=(field, field), in_specs=[vmem] * 5, out...  30.9 us
    pallas_call x2, Pallas kernels, east_sums(): pl.pallas_call(east_kernel, grid=(groups,), in_specs=[strip_spec(3, start...  12.5 us
    pallas_call x1, Pallas kernels, south_sums(): pl.pallas_call(south_kernel, grid=(groups,), in_specs=[strip_spec(2), str...  11.7 us
    ppermute x3, waiting for transfers between devices, passed_along(): return lax.ppermute(x, axis, pairs)  5.97 us
    pallas_call x2, Pallas kernels, pack_left(): pl.pallas_call(pack_kernel, grid=(groups,), in_specs=[strip_spec(0, start...  5.43 us
    ppermute x3, starting transfers between devices, passed_along(): return lax.ppermute(x, axis, pairs)  3.86 us
    unnamed x32, local copies, waits for them, and re-layouts  3.74 us
    reshape x2, local copies, waits for them, and re-layouts, by_tile(): return field.reshape(2, tile_count, nodes).transpose(1, 0, 2)[:, None]  1.72 us
  transfers between devices with their start and end apart: 3, of which 2 were waited for; matrix products, arithmetic and copies ran while one was open for 10% of the time, Pallas kernels for 25%

profile of v2, /device:TPU:0, one launch (start us, length us, event | category | flops | bytes accessed | tf_op | source)
XLA Modules:
  0.0 84.4 jit_solution(10260543132179085215)
XLA Ops:
  0.7 3.3 %shard_map.131 = bf16[12,64,640]{2,1,0:T(8,128)(2,1)S(1)} custom-call(bf16[40,1,4,64,512]{4,3,2,1,0:T(8,128)(2,1)} %below_ref.1), custom_call_target="tpu_custom_call" | custom-call | tf_op jit(solution)/shard_map/pallas_call | solution.py:136
  4.0 1.3 %collective-permute-start.1 = (bf16[12,64,640]{2,1,0:T(8,128)(2,1)S(1)}, bf16[12,64,640]{2,1,0:T(8,128)(2,1)S(1)}, u32[]{:S(2)}, u32[]{:S(2)}) collective-permute-start(bf16[12,64,640]{2,1,0:T(8,128)(2,1)S(1)} %shard_map.131), channel_id=1, source_target_pairs={{4,0},{8,4},{12,8},{16,12},{20,16},{24,20},{28,24},{5,1},{9,5},{13... | collective-permute-start | bytes 2949128 | tf_op jit(solution)/shard_map/ppermute | solution.py:189
  5.3 2.2 %shard_map.130 = bf16[8,64,640]{2,1,0:T(8,128)(2,1)S(1)} custom-call(bf16[40,1,4,64,512]{4,3,2,1,0:T(8,128)(2,1)} %below_ref.1), custom_call_target="tpu_custom_call" | custom-call | tf_op jit(solution)/shard_map/pallas_call | solution.py:136
  7.4 1.3 %collective-permute-start = (bf16[8,64,640]{2,1,0:T(8,128)(2,1)S(1)}, bf16[8,64,640]{2,1,0:T(8,128)(2,1)S(1)}, u32[]{:S(2)}, u32[]{:S(2)}) collective-permute-start(bf16[8,64,640]{2,1,0:T(8,128)(2,1)S(1)} %shard_map.130), channel_id=1, source_target_pairs={{4,0},{8,4},{12,8},{16,12},{20,16},{24,20},{28,24},{5,1},{9,5},{13... | collective-permute-start | bytes 1966088 | tf_op jit(solution)/shard_map/ppermute | solution.py:189
  8.7 1.4 %slice_bitcast_fusion = bf16[1,64,384]{2,1,0:T(8,128)(2,1)} fusion(bf16[40,1,4,64,512]{4,3,2,1,0:T(8,128)(2,1)} %below_ref.1), kind=kLoop, calls=%fused_computation.5 | loop fusion | bytes 98304 | tf_op jit(solution)/shard_map/squeeze | solution.py:468
  10.2 1.3 %collective-permute-start.2 = (bf16[1,64,384]{2,1,0:T(8,128)(2,1)}, bf16[1,64,384]{2,1,0:T(8,128)(2,1)}, u32[]{:S(2)}, u32[]{:S(2)}) collective-permute-start(bf16[1,64,384]{2,1,0:T(8,128)(2,1)} %slice_bitcast_fusion), channel_id=1, source_target_pairs={{1,0},{2,1},{3,2},{5,4},{6,5},{7,6},{9,8},{10,9},{11,10},{13,12},{... | collective-permute-start | bytes 147464 | tf_op jit(solution)/shard_map/ppermute | solution.py:189
  11.5 0.6 iota_compare_fusion
  12.0 0.6 convert_bitcast_fusion
  12.6 0.6 iota_compare_fusion.1
  13.2 1.4 %copy.26 = f32[40,2]{1,0:T(8,128)} copy(f32[40,2]{0,1:T(2,128)} %convert_bitcast_fusion) | data formatting | bytes 640 | tf_op jit(solution)/shard_map/convert_element_type | solution.py:487
  14.5 0.7 pad.13.clone
  15.2 0.6 pad.2.clone
  15.8 1.6 %copy.36 = f32[40,1,896]{2,0,1:T(8,128)} copy(f32[40,1,896]{2,1,0:T(1,128)} %param.15) | data formatting | bytes 286720
  17.4 1.3 %copy.27.refs_1_ = f32[40,1]{1,0:T(8,128)} copy(f32[40,1]{0,1:T(1,128)} %param.14) | data formatting | bytes 320 | tf_op args[3]
  18.8 0.7 copy-done.3
  19.5 11.7 %shard_map.134 = f32[10,10,128]{2,1,0:T(8,128)S(1)} custom-call(bf16[40,1,4,64,512]{4,3,2,1,0:T(8,128)(2,1)} %below_ref.1, bf16[40,1,4,64,512]{4,3,2,1,0:T(8,128)(2,1)} %below_ref.1, bf16[40,1,4,64,512]{4,3,2,1,0:T(8,128)(2,1)} %below_ref.1, bf16[1,64,384]{2,1,0:T(8,128)(2,1)} %collective-permute-done.2.next_ref, bf16[128,64]{1,0:T(8,128)(2,1)S(1)} %copy-done.3, ...), custom_call_target="tpu_custom_call" | custom-call | flops 3000000000 | bytes 4000000 | tf_op jit(solution)/shard_map/pallas_call | solution.py:153
  31.2 0.2 collective-permute-done.1.second_ref
  31.5 7.4 %shard_map.132 = f32[6,10,128]{2,1,0:T(8,128)S(1)} custom-call(bf16[40,1,4,64,512]{4,3,2,1,0:T(8,128)(2,1)} %below_ref.1, bf16[12,64,640]{2,1,0:T(8,128)(2,1)S(1)} %collective-permute-done.1.second_ref, bf16[128,64]{1,0:T(8,128)(2,1)S(1)} %copy-done.3, bf16[256,256]{1,0:T(8,128)(2,1)S(1)} %copy-done.1, bf16[256,256]{1,0:T(8,128)(2,1)S(1)} %copy-done, ...), custom_call_target="tpu_custom_call" | custom-call | flops 1800000000 | bytes 2400000 | tf_op jit(solution)/shard_map/pallas_call | solution.py:167
  38.8 5.8 %collective-permute-done.second_ref = bf16[8,64,640]{2,1,0:T(8,128)(2,1)S(1)} collective-permute-done((bf16[8,64,640]{2,1,0:T(8,128)(2,1)S(1)}, bf16[8,64,640]{2,1,0:T(8,128)(2,1)S(1)}, u32[]{:S(2)}, u32[]{:S(2)}) %collective-permute-start) | collective-permute-done | bytes 655392 | tf_op jit(solution)/shard_map/ppermute | solution.py:189
  44.6 5.1 %shard_map.133 = f32[4,10,128]{2,1,0:T(8,128)S(1)} custom-call(bf16[40,1,4,64,512]{4,3,2,1,0:T(8,128)(2,1)} %below_ref.1, bf16[8,64,640]{2,1,0:T(8,128)(2,1)S(1)} %collective-permute-done.second_ref, bf16[128,64]{1,0:T(8,128)(2,1)S(1)} %copy-done.3, bf16[256,256]{1,0:T(8,128)(2,1)S(1)} %copy-done.1, bf16[256,256]{1,0:T(8,128)(2,1)S(1)} %copy-done, ...), custom_call_target="tpu_custom_call" | custom-call | flops 1200000000 | bytes 1600000 | tf_op jit(solution)/shard_map/pallas_call | solution.py:167
  49.8 0.2 copy.21
  50.0 0.3 copy.22
  50.3 0.3 reshape.160
  50.6 0.1 copy.23
  50.7 0.1 reshape.165
  50.8 0.1 maximum_maximum_fusion.1
  50.9 0.1 slice_bitcast_fusion.3
  51.0 0.6 pad_maximum_fusion.2
  51.7 0.1 maximum_maximum_fusion.refs_0_
  51.8 30.9 %shard_map.135 = (f32[80,896]{1,0:T(8,128)S(1)}, f32[80,896]{1,0:T(8,128)S(1)}) custom-call(f32[40,128]{1,0:T(8,128)S(1)} %maximum_maximum_fusion.refs_0_, f32[40,1]{1,0:T(8,128)S(1)} %copy-done.7, f32[40,896]{1,0:T(8,128)S(1)} %bitcast.50, bf16[896,128]{1,0:T(8,128)(2,1)S(1)} %copy-done.4, bf16[128,896]{1,0:T(8,128)(2,1)S(1)} %copy-done.5), custom_call_target="tpu_custom_call" | custom-call | tf_op jit(solution)/shard_map/pallas_call | solution.py:427
  82.7 0.9 %copy.34 = f32[2,40,896]{2,0,1:T(2,128)} copy(f32[2,40,896]{2,1,0:T(8,128)S(1)} %bitcast.52) | data formatting | bytes 573440 | tf_op jit(solution)/shard_map/reshape | solution.py:496
  83.6 0.9 %copy.35 = f32[2,40,896]{2,0,1:T(2,128)} copy(f32[2,40,896]{2,1,0:T(8,128)S(1)} %bitcast.51) | data formatting | bytes 573440 | tf_op jit(solution)/shard_map/reshape | solution.py:496
  (39 shorter events, 0.2 us)
Async XLA Ops:
  0.6 18.1 %copy-start = (bf16[256,256]{1,0:T(8,128)(2,1)S(1)}, bf16[256,256]{1,0:T(8,128)(2,1)}, u32[]{:S(2)}) copy-start(bf16[256,256]{1,0:T(8,128)(2,1)} %constant.20.clone.bl_ref) | copy-start | bytes 393220
  0.6 18.1 %copy-start.1 = (bf16[256,256]{1,0:T(8,128)(2,1)S(1)}, bf16[256,256]{1,0:T(8,128)(2,1)}, u32[]{:S(2)}) copy-start(bf16[256,256]{1,0:T(8,128)(2,1)} %constant.7.clone.l_ref) | copy-start | bytes 393220
  0.7 18.1 %copy-start.6 = (bf16[64,128]{1,0:T(8,128)(2,1)S(1)}, bf16[64,128]{1,0:T(8,128)(2,1)}, u32[]{:S(2)}) copy-start(bf16[64,128]{1,0:T(8,128)(2,1)} %constant.21.clone.bd_ref) | copy-start | bytes 49156
  0.7 10.8 %copy-start.11 = (s32[40,1,2]{0,2,1:T(2,128)S(1)}, s32[40,1,2]{0,2,1:T(2,128)}, u32[]{:S(2)}) copy-start(s32[40,1,2]{0,2,1:T(2,128)} %param.12) | copy-start | bytes 964
  0.7 11.4 %copy-start.12 = (s32[40,1,2]{0,2,1:T(2,128)S(1)}, s32[40,1,2]{0,2,1:T(2,128)}, u32[]{:S(2)}) copy-start(s32[40,1,2]{0,2,1:T(2,128)} %param.13) | copy-start | bytes 964
  4.0 27.4 %collective-permute-start.1 = (bf16[12,64,640]{2,1,0:T(8,128)(2,1)S(1)}, bf16[12,64,640]{2,1,0:T(8,128)(2,1)S(1)}, u32[]{:S(2)}, u32[]{:S(2)}) collective-permute-start(bf16[12,64,640]{2,1,0:T(8,128)(2,1)S(1)} %shard_map.131), channel_id=1, source_target_pairs={{4,0},{8,4},{12,8},{16,12},{20,16},{24,20},{28,24},{5,1},{9,5},{13... | collective-permute-start | bytes 2949128 | tf_op jit(solution)/shard_map/ppermute | solution.py:189
  7.4 37.2 %collective-permute-start = (bf16[8,64,640]{2,1,0:T(8,128)(2,1)S(1)}, bf16[8,64,640]{2,1,0:T(8,128)(2,1)S(1)}, u32[]{:S(2)}, u32[]{:S(2)}) collective-permute-start(bf16[8,64,640]{2,1,0:T(8,128)(2,1)S(1)} %shard_map.130), channel_id=1, source_target_pairs={{4,0},{8,4},{12,8},{16,12},{20,16},{24,20},{28,24},{5,1},{9,5},{13... | collective-permute-start | bytes 1966088 | tf_op jit(solution)/shard_map/ppermute | solution.py:189
  10.2 8.6 %collective-permute-start.2 = (bf16[1,64,384]{2,1,0:T(8,128)(2,1)}, bf16[1,64,384]{2,1,0:T(8,128)(2,1)}, u32[]{:S(2)}, u32[]{:S(2)}) collective-permute-start(bf16[1,64,384]{2,1,0:T(8,128)(2,1)} %slice_bitcast_fusion), channel_id=1, source_target_pairs={{1,0},{2,1},{3,2},{5,4},{6,5},{7,6},{9,8},{10,9},{11,10},{13,12},{... | collective-permute-start | bytes 147464 | tf_op jit(solution)/shard_map/ppermute | solution.py:189
  18.8 0.8 copy-start.3
  31.4 19.4 %copy-start.14 = (f32[8]{0:T(128)S(1)}, f32[8]{0:T(128)}, u32[]{:S(2)}) copy-start(f32[8]{0:T(128)} %pad.13.clone) | copy-start | bytes 100
  31.4 19.6 %copy-start.9 = (pred[40,8]{0,1:T(8,128)(4,1)S(1)}, pred[40,8]{0,1:T(8,128)(4,1)}, u32[]{:S(2)}) copy-start(pred[40,8]{0,1:T(8,128)(4,1)} %iota_compare_fusion) | copy-start | bytes 964
  31.4 19.6 %copy-start.10 = (pred[40,8]{0,1:T(8,128)(4,1)S(1)}, pred[40,8]{0,1:T(8,128)(4,1)}, u32[]{:S(2)}) copy-start(pred[40,8]{0,1:T(8,128)(4,1)} %iota_compare_fusion.1) | copy-start | bytes 964
  31.4 20.3 %copy-start.8 = (f32[40,2]{1,0:T(8,128)S(1)}, f32[40,2]{1,0:T(8,128)}, u32[]{:S(2)}) copy-start(f32[40,2]{1,0:T(8,128)} %copy.26) | copy-start | bytes 964
  31.4 20.3 %copy-start.13 = (f32[128]{0:T(128)S(1)}, f32[128]{0:T(128)}, u32[]{:S(2)}) copy-start(f32[128]{0:T(128)} %pad.2.clone) | copy-start | bytes 1540
  31.4 20.4 %copy-start.2 = (f32[40,1,896]{2,0,1:T(8,128)S(1)}, f32[40,1,896]{2,0,1:T(8,128)}, u32[]{:S(2)}) copy-start(f32[40,1,896]{2,0,1:T(8,128)} %copy.36) | copy-start | bytes 430084
  31.4 20.4 %copy-start.4 = (bf16[896,128]{1,0:T(8,128)(2,1)S(1)}, bf16[896,128]{1,0:T(8,128)(2,1)}, u32[]{:S(2)}) copy-start(bf16[896,128]{1,0:T(8,128)(2,1)} %constant.22.clone.refs_3_) | copy-start | bytes 688132
  31.4 20.4 %copy-start.5 = (bf16[128,896]{1,0:T(8,128)(2,1)S(1)}, bf16[128,896]{1,0:T(8,128)(2,1)}, u32[]{:S(2)}) copy-start(bf16[128,896]{1,0:T(8,128)(2,1)} %constant.23.clone.refs_4_) | copy-start | bytes 688132
  31.5 20.4 %copy-start.7 = (f32[40,1]{1,0:T(8,128)S(1)}, f32[40,1]{1,0:T(8,128)}, u32[]{:S(2)}) copy-start(f32[40,1]{1,0:T(8,128)} %copy.27.refs_1_) | copy-start | bytes 484

commit v3 on v2

--- a/solution.py
+++ b/solution.py
@@ -101,8 +101,8 @@
 
 
 def pack_kernel(left_ref, out_ref):
-    out_ref[0] = pack_two(left_ref[0], left_ref[1])
-    out_ref[1] = pack_two(left_ref[2], left_ref[3])
+    for pair in range(GROUP):
+        out_ref[pair] = pack_two(left_ref[2 * pair], left_ref[2 * pair + 1])
 
 
 def strip_spec(side, start=0):
@@ -135,9 +135,9 @@
 def pack_left(strips, start, groups):
     return pl.pallas_call(
         pack_kernel,
-        grid=(groups,),
-        in_specs=[strip_spec(0, start)],
-        out_specs=pl.BlockSpec((2, PATCH, PACKED), lambda i: (i, 0, 0)),
+        grid=(groups // 2,),
+        in_specs=[pl.BlockSpec((2 * GROUP, None, None, PATCH, WIDE), lambda i: (i + start // 2, 0, 0, 0, 0))],
+        out_specs=pl.BlockSpec((GROUP, PATCH, PACKED), lambda i: (i, 0, 0)),
         out_shape=jax.ShapeDtypeStruct((2 * groups, PATCH, PACKED), jnp.bfloat16),
         compiler_params=PARAMS,
     )(strips)
@@ -486,7 +486,7 @@
     match_terms = jnp.stack([east_terms, south_terms], axis=1)
     offsets = pair_offsets[:, 0].astype(jnp.float32)
     table = jnp.concatenate(
-        [match_terms.reshape(tile_count, 6 * blocks), offsets, jnp.zeros((tile_count, 126 - 6 * blocks), jnp.float32)],
+        [match_terms.reshape(tile_count, 6 * blocks), offsets],
         axis=1,
     )
     positions, residual = mesh_solve(table, tile_stiffness, anchor[:, 0])

time: 85 us -> 84 us (0.988)
  Pallas kernels: 60.5 us -> 58.7 us
  waiting for transfers between devices: 5.97 us -> 7.52 us
    pallas_call x2, Pallas kernels: 5.43 us -> 3.62 us  [pack_left(): pl.pallas_call(pack_kernel, grid=(groups // 2,), in_specs=[pl.BlockSpec((...]
    ppermute x3, waiting for transfers between devices: 5.97 us -> 7.52 us  [passed_along(): return lax.ppermute(x, axis, pairs)]
    unnamed x32 -> x30, local copies, waits for them, and re-layouts: 3.74 us -> 3.73 us
  transfers between devices with their start and end apart: 3 -> 3, of which waited for: 2 -> 2; matrix products, arithmetic and copies ran while one was open for 10% -> 10% of each run, Pallas kernels for 25% -> 24%
where the time goes in v3:
time: 84 us; the launch traced here: 83.5 us
  Pallas kernels  58.7 us (70%)
  local copies, waits for them, and re-layouts  9.94 us (12%)
  waiting for transfers between devices  7.52 us (9%)
  starting transfers between devices  3.86 us (5%)
  other arithmetic  2.59 us (3%)
  between operations  0.89 us (1%)
    pallas_call x1, Pallas kernels, mesh_solve(): pl.pallas_call(kernel, out_shape=(field, field), in_specs=[vmem] * 5, out...  30.9 us
    pallas_call x2, Pallas kernels, east_sums(): pl.pallas_call(east_kernel, grid=(groups,), in_specs=[strip_spec(3, start...  12.5 us
    pallas_call x1, Pallas kernels, south_sums(): pl.pallas_call(south_kernel, grid=(groups,), in_specs=[strip_spec(2), str...  11.7 us
    ppermute x3, waiting for transfers between devices, passed_along(): return lax.ppermute(x, axis, pairs)  7.52 us
    ppermute x3, starting transfers between devices, passed_along(): return lax.ppermute(x, axis, pairs)  3.86 us
    unnamed x30, local copies, waits for them, and re-layouts  3.73 us
    pallas_call x2, Pallas kernels, pack_left(): pl.pallas_call(pack_kernel, grid=(groups // 2,), in_specs=[pl.BlockSpec((...  3.62 us
    reshape x2, local copies, waits for them, and re-layouts, by_tile(): return field.reshape(2, tile_count, nodes).transpose(1, 0, 2)[:, None]  1.72 us
  transfers between devices with their start and end apart: 3, of which 2 were waited for; matrix products, arithmetic and copies ran while one was open for 10% of the time, Pallas kernels for 24%

profile of v3, /device:TPU:0, one launch (start us, length us, event | category | flops | bytes accessed | tf_op | source)
XLA Modules:
  0.0 83.5 jit_solution(5003233757865682663)
XLA Ops:
  0.7 2.4 %shard_map.131 = bf16[12,64,640]{2,1,0:T(8,128)(2,1)S(1)} custom-call(bf16[40,1,4,64,512]{4,3,2,1,0:T(8,128)(2,1)} %below_ref.1), custom_call_target="tpu_custom_call" | custom-call | tf_op jit(solution)/shard_map/pallas_call | solution.py:136
  3.1 1.3 %collective-permute-start.1 = (bf16[12,64,640]{2,1,0:T(8,128)(2,1)S(1)}, bf16[12,64,640]{2,1,0:T(8,128)(2,1)S(1)}, u32[]{:S(2)}, u32[]{:S(2)}) collective-permute-start(bf16[12,64,640]{2,1,0:T(8,128)(2,1)S(1)} %shard_map.131), channel_id=1, source_target_pairs={{4,0},{8,4},{12,8},{16,12},{20,16},{24,20},{28,24},{5,1},{9,5},{13... | collective-permute-start | bytes 2949128 | tf_op jit(solution)/shard_map/ppermute | solution.py:189
  4.4 1.3 %shard_map.130 = bf16[8,64,640]{2,1,0:T(8,128)(2,1)S(1)} custom-call(bf16[40,1,4,64,512]{4,3,2,1,0:T(8,128)(2,1)} %below_ref.1), custom_call_target="tpu_custom_call" | custom-call | tf_op jit(solution)/shard_map/pallas_call | solution.py:136
  5.6 1.3 %collective-permute-start = (bf16[8,64,640]{2,1,0:T(8,128)(2,1)S(1)}, bf16[8,64,640]{2,1,0:T(8,128)(2,1)S(1)}, u32[]{:S(2)}, u32[]{:S(2)}) collective-permute-start(bf16[8,64,640]{2,1,0:T(8,128)(2,1)S(1)} %shard_map.130), channel_id=1, source_target_pairs={{4,0},{8,4},{12,8},{16,12},{20,16},{24,20},{28,24},{5,1},{9,5},{13... | collective-permute-start | bytes 1966088 | tf_op jit(solution)/shard_map/ppermute | solution.py:189
  6.9 1.4 %slice_bitcast_fusion = bf16[1,64,384]{2,1,0:T(8,128)(2,1)} fusion(bf16[40,1,4,64,512]{4,3,2,1,0:T(8,128)(2,1)} %below_ref.1), kind=kLoop, calls=%fused_computation.5 | loop fusion | bytes 98304 | tf_op jit(solution)/shard_map/squeeze | solution.py:468
  8.3 1.3 %collective-permute-start.2 = (bf16[1,64,384]{2,1,0:T(8,128)(2,1)}, bf16[1,64,384]{2,1,0:T(8,128)(2,1)}, u32[]{:S(2)}, u32[]{:S(2)}) collective-permute-start(bf16[1,64,384]{2,1,0:T(8,128)(2,1)} %slice_bitcast_fusion), channel_id=1, source_target_pairs={{1,0},{2,1},{3,2},{5,4},{6,5},{7,6},{9,8},{10,9},{11,10},{13,12},{... | collective-permute-start | bytes 147464 | tf_op jit(solution)/shard_map/ppermute | solution.py:189
  9.7 0.6 iota_compare_fusion
  10.3 0.6 convert_bitcast_fusion
  10.8 0.6 iota_compare_fusion.1
  11.4 1.4 %copy.26 = f32[40,2]{1,0:T(8,128)} copy(f32[40,2]{0,1:T(2,128)} %convert_bitcast_fusion) | data formatting | bytes 640 | tf_op jit(solution)/shard_map/convert_element_type | solution.py:487
  12.8 1.6 %copy.36 = f32[40,1,896]{2,0,1:T(8,128)} copy(f32[40,1,896]{2,1,0:T(1,128)} %param.15) | data formatting | bytes 286720
  14.3 1.3 %copy.27.refs_1_ = f32[40,1]{1,0:T(8,128)} copy(f32[40,1]{0,1:T(1,128)} %param.14) | data formatting | bytes 320 | tf_op args[3]
  15.7 0.6 pad.12.clone
  16.3 0.7 copy-done.3
  17.1 11.7 %shard_map.134 = f32[10,10,128]{2,1,0:T(8,128)S(1)} custom-call(bf16[40,1,4,64,512]{4,3,2,1,0:T(8,128)(2,1)} %below_ref.1, bf16[40,1,4,64,512]{4,3,2,1,0:T(8,128)(2,1)} %below_ref.1, bf16[40,1,4,64,512]{4,3,2,1,0:T(8,128)(2,1)} %below_ref.1, bf16[1,64,384]{2,1,0:T(8,128)(2,1)} %collective-permute-done.2.next_ref, bf16[128,64]{1,0:T(8,128)(2,1)S(1)} %copy-done.3, ...), custom_call_target="tpu_custom_call" | custom-call | flops 3000000000 | bytes 4000000 | tf_op jit(solution)/shard_map/pallas_call | solution.py:153
  28.7 1.7 %collective-permute-done.1.second_ref = bf16[12,64,640]{2,1,0:T(8,128)(2,1)S(1)} collective-permute-done((bf16[12,64,640]{2,1,0:T(8,128)(2,1)S(1)}, bf16[12,64,640]{2,1,0:T(8,128)(2,1)S(1)}, u32[]{:S(2)}, u32[]{:S(2)}) %collective-permute-start.1) | collective-permute-done | bytes 983072 | tf_op jit(solution)/shard_map/ppermute | solution.py:189
  30.5 7.4 %shard_map.132 = f32[6,10,128]{2,1,0:T(8,128)S(1)} custom-call(bf16[40,1,4,64,512]{4,3,2,1,0:T(8,128)(2,1)} %below_ref.1, bf16[12,64,640]{2,1,0:T(8,128)(2,1)S(1)} %collective-permute-done.1.second_ref, bf16[128,64]{1,0:T(8,128)(2,1)S(1)} %copy-done.3, bf16[256,256]{1,0:T(8,128)(2,1)S(1)} %copy-done, bf16[256,256]{1,0:T(8,128)(2,1)S(1)} %copy-done.1, ...), custom_call_target="tpu_custom_call" | custom-call | flops 1800000000 | bytes 2400000 | tf_op jit(solution)/shard_map/pallas_call | solution.py:167
  37.9 5.8 %collective-permute-done.second_ref = bf16[8,64,640]{2,1,0:T(8,128)(2,1)S(1)} collective-permute-done((bf16[8,64,640]{2,1,0:T(8,128)(2,1)S(1)}, bf16[8,64,640]{2,1,0:T(8,128)(2,1)S(1)}, u32[]{:S(2)}, u32[]{:S(2)}) %collective-permute-start) | collective-permute-done | bytes 655392 | tf_op jit(solution)/shard_map/ppermute | solution.py:189
  43.7 5.1 %shard_map.133 = f32[4,10,128]{2,1,0:T(8,128)S(1)} custom-call(bf16[40,1,4,64,512]{4,3,2,1,0:T(8,128)(2,1)} %below_ref.1, bf16[8,64,640]{2,1,0:T(8,128)(2,1)S(1)} %collective-permute-done.second_ref, bf16[128,64]{1,0:T(8,128)(2,1)S(1)} %copy-done.3, bf16[256,256]{1,0:T(8,128)(2,1)S(1)} %copy-done, bf16[256,256]{1,0:T(8,128)(2,1)S(1)} %copy-done.1, ...), custom_call_target="tpu_custom_call" | custom-call | flops 1200000000 | bytes 1600000 | tf_op jit(solution)/shard_map/pallas_call | solution.py:167
  48.9 0.2 copy.21
  49.1 0.3 copy.22
  49.3 0.3 reshape.160
  49.6 0.1 copy.23
  49.8 0.1 reshape.165
  49.9 0.1 maximum_maximum_fusion
  50.0 0.1 slice_bitcast_fusion.3
  50.1 0.6 pad_maximum_fusion.2
  50.7 0.1 copy.25
  50.8 0.1 pad_maximum_fusion.3.refs_0_
  50.9 30.9 %shard_map.135 = (f32[80,896]{1,0:T(8,128)S(1)}, f32[80,896]{1,0:T(8,128)S(1)}) custom-call(f32[40,50]{1,0:T(8,128)S(1)} %pad_maximum_fusion.3.refs_0_, f32[40,1]{1,0:T(8,128)S(1)} %copy-done.7, f32[40,896]{1,0:T(8,128)S(1)} %bitcast.50, bf16[896,128]{1,0:T(8,128)(2,1)S(1)} %copy-done.4, bf16[128,896]{1,0:T(8,128)(2,1)S(1)} %copy-done.5), custom_call_target="tpu_custom_call" | custom-call | tf_op jit(solution)/shard_map/pallas_call | solution.py:427
  81.8 0.9 %copy.34 = f32[2,40,896]{2,0,1:T(2,128)} copy(f32[2,40,896]{2,1,0:T(8,128)S(1)} %bitcast.52) | data formatting | bytes 573440 | tf_op jit(solution)/shard_map/reshape | solution.py:496
  82.6 0.9 %copy.35 = f32[2,40,896]{2,0,1:T(2,128)} copy(f32[2,40,896]{2,1,0:T(8,128)S(1)} %bitcast.51) | data formatting | bytes 573440 | tf_op jit(solution)/shard_map/reshape | solution.py:496
  (35 shorter events, 0.1 us)
Async XLA Ops:
  0.6 15.7 %copy-start = (bf16[256,256]{1,0:T(8,128)(2,1)S(1)}, bf16[256,256]{1,0:T(8,128)(2,1)}, u32[]{:S(2)}) copy-start(bf16[256,256]{1,0:T(8,128)(2,1)} %constant.18.clone.l_ref) | copy-start | bytes 393220
  0.6 15.6 %copy-start.1 = (bf16[256,256]{1,0:T(8,128)(2,1)S(1)}, bf16[256,256]{1,0:T(8,128)(2,1)}, u32[]{:S(2)}) copy-start(bf16[256,256]{1,0:T(8,128)(2,1)} %constant.19.clone.bl_ref) | copy-start | bytes 393220
  0.7 15.6 %copy-start.6 = (bf16[64,128]{1,0:T(8,128)(2,1)S(1)}, bf16[64,128]{1,0:T(8,128)(2,1)}, u32[]{:S(2)}) copy-start(bf16[64,128]{1,0:T(8,128)(2,1)} %constant.20.clone.bd_ref) | copy-start | bytes 49156
  0.7 9.0 %copy-start.11 = (s32[40,1,2]{0,2,1:T(2,128)S(1)}, s32[40,1,2]{0,2,1:T(2,128)}, u32[]{:S(2)}) copy-start(s32[40,1,2]{0,2,1:T(2,128)} %param.12) | copy-start | bytes 964
  0.7 9.6 %copy-start.12 = (s32[40,1,2]{0,2,1:T(2,128)S(1)}, s32[40,1,2]{0,2,1:T(2,128)}, u32[]{:S(2)}) copy-start(s32[40,1,2]{0,2,1:T(2,128)} %param.13) | copy-start | bytes 964
  3.1 27.4 %collective-permute-start.1 = (bf16[12,64,640]{2,1,0:T(8,128)(2,1)S(1)}, bf16[12,64,640]{2,1,0:T(8,128)(2,1)S(1)}, u32[]{:S(2)}, u32[]{:S(2)}) collective-permute-start(bf16[12,64,640]{2,1,0:T(8,128)(2,1)S(1)} %shard_map.131), channel_id=1, source_target_pairs={{4,0},{8,4},{12,8},{16,12},{20,16},{24,20},{28,24},{5,1},{9,5},{13... | collective-permute-start | bytes 2949128 | tf_op jit(solution)/shard_map/ppermute | solution.py:189
  5.6 38.1 %collective-permute-start = (bf16[8,64,640]{2,1,0:T(8,128)(2,1)S(1)}, bf16[8,64,640]{2,1,0:T(8,128)(2,1)S(1)}, u32[]{:S(2)}, u32[]{:S(2)}) collective-permute-start(bf16[8,64,640]{2,1,0:T(8,128)(2,1)S(1)} %shard_map.130), channel_id=1, source_target_pairs={{4,0},{8,4},{12,8},{16,12},{20,16},{24,20},{28,24},{5,1},{9,5},{13... | collective-permute-start | bytes 1966088 | tf_op jit(solution)/shard_map/ppermute | solution.py:189
  8.3 7.9 %collective-permute-start.2 = (bf16[1,64,384]{2,1,0:T(8,128)(2,1)}, bf16[1,64,384]{2,1,0:T(8,128)(2,1)}, u32[]{:S(2)}, u32[]{:S(2)}) collective-permute-start(bf16[1,64,384]{2,1,0:T(8,128)(2,1)} %slice_bitcast_fusion), channel_id=1, source_target_pairs={{1,0},{2,1},{3,2},{5,4},{6,5},{7,6},{9,8},{10,9},{11,10},{13,12},{... | collective-permute-start | bytes 147464 | tf_op jit(solution)/shard_map/ppermute | solution.py:189
  16.3 0.8 copy-start.3
  30.5 19.4 %copy-start.13 = (f32[8]{0:T(128)S(1)}, f32[8]{0:T(128)}, u32[]{:S(2)}) copy-start(f32[8]{0:T(128)} %pad.12.clone) | copy-start | bytes 100
  30.5 19.6 %copy-start.9 = (pred[40,8]{0,1:T(8,128)(4,1)S(1)}, pred[40,8]{0,1:T(8,128)(4,1)}, u32[]{:S(2)}) copy-start(pred[40,8]{0,1:T(8,128)(4,1)} %iota_compare_fusion) | copy-start | bytes 964
  30.5 19.6 %copy-start.10 = (pred[40,8]{0,1:T(8,128)(4,1)S(1)}, pred[40,8]{0,1:T(8,128)(4,1)}, u32[]{:S(2)}) copy-start(pred[40,8]{0,1:T(8,128)(4,1)} %iota_compare_fusion.1) | copy-start | bytes 964
  30.5 20.3 %copy-start.8 = (f32[40,2]{1,0:T(8,128)S(1)}, f32[40,2]{1,0:T(8,128)}, u32[]{:S(2)}) copy-start(f32[40,2]{1,0:T(8,128)} %copy.26) | copy-start | bytes 964
  30.5 20.4 %copy-start.2 = (f32[40,1,896]{2,0,1:T(8,128)S(1)}, f32[40,1,896]{2,0,1:T(8,128)}, u32[]{:S(2)}) copy-start(f32[40,1,896]{2,0,1:T(8,128)} %copy.36) | copy-start | bytes 430084
  30.5 20.4 %copy-start.4 = (bf16[896,128]{1,0:T(8,128)(2,1)S(1)}, bf16[896,128]{1,0:T(8,128)(2,1)}, u32[]{:S(2)}) copy-start(bf16[896,128]{1,0:T(8,128)(2,1)} %constant.21.clone.refs_3_) | copy-start | bytes 688132
  30.5 20.4 %copy-start.5 = (bf16[128,896]{1,0:T(8,128)(2,1)S(1)}, bf16[128,896]{1,0:T(8,128)(2,1)}, u32[]{:S(2)}) copy-start(bf16[128,896]{1,0:T(8,128)(2,1)} %constant.22.clone.refs_4_) | copy-start | bytes 688132
  30.5 20.4 %copy-start.7 = (f32[40,1]{1,0:T(8,128)S(1)}, f32[40,1]{1,0:T(8,128)}, u32[]{:S(2)}) copy-start(f32[40,1]{1,0:T(8,128)} %copy.27.refs_1_) | copy-start | bytes 484
